TPU v7x, 32 devices: a whole 2x2x4 slice. The times are simulated.
32 devices in a mesh: dp: 16 (over z, y, x), head: 2 (over core).
Axes of the slice: x: 2, y: 2, z: 4, core: 2. Of those that a mesh axis runs over, the one named last changes fastest.
Arguments:
- queries: bfloat16 [2048, 12288], P('dp', 'head'), may hold values from -128 to 128
- keys: bfloat16 [2048, 1024], P('dp', 'head'), may hold values from -6 to 6
- values: bfloat16 [2048, 1024], P('dp', 'head'), may hold values from -6 to 6
- grad_out: bfloat16 [2048, 12288], P(('dp', 'head')), may hold values from -6 to 6
- segments: int32 [2048], replicated, may hold values from 0 to 3, never falling along the last dimension, each value on 1 to 1024 neighbouring positions
Outputs:
- attention_out: bfloat16 [2048, 12288], P(('dp', 'head'))
- grad_queries: bfloat16 [2048, 12288], P('dp', 'head')
- grad_keys: bfloat16 [2048, 1024], P('dp', 'head')
- grad_values: bfloat16 [2048, 1024], P('dp', 'head')
Inputs may be any that keep to these rules, and one draw needn't show every extreme that they name: segments never fall; each document holds 1 to 1024 tokens and one holds exactly 1024.
All inputs are finite; a program needn't handle non-finite values.
Results may differ from a plain program's by a relative error of at most 0.011.
Values may be sent and summed in bfloat16 or wider, within the bound.
A program may use at most 128 MiB of HBM per device.

v0:
```python
import math

import jax
import jax.numpy as jnp
from jax import lax
from jax.sharding import PartitionSpec as P

QHEADS = 96
KVHEADS = 8
HEAD_DIM = 128
DEPTH = 8


def from_behind(value, axis, steps):
    count = lax.axis_size(axis)
    first, last = (max(0, -steps), min(count, count - steps))
    return lax.ppermute(value, axis, [(source, source + steps) for source in range(first, last)])


def attend(query_heads, cotangent_heads, key_blocks, value_blocks, allowed_blocks):
    head_size = query_heads.shape[2]
    softmax_scale = 1.0 / math.sqrt(head_size)
    raw_scores = jnp.einsum(
        "rgd,jwd->jgrw", query_heads, key_blocks, preferred_element_type=jnp.float32
    )
    scores = jnp.where(allowed_blocks[:, None], softmax_scale * raw_scores, -jnp.inf)
    row_max = jnp.max(scores, axis=(0, 3), keepdims=True)
    exp_total = jnp.sum(jnp.exp(scores - row_max), axis=(0, 3), keepdims=True)
    log_total = row_max + jnp.log(exp_total)
    weights = jnp.exp(scores - log_total)
    weights_low = weights.astype(jnp.bfloat16)
    out_heads = jnp.einsum(
        "jgrw,jwd->rgd", weights_low, value_blocks, preferred_element_type=jnp.float32
    )
    out_low = lax.optimization_barrier(out_heads.astype(jnp.bfloat16))
    row_delta = jnp.sum(cotangent_heads.astype(jnp.float32) * out_low.astype(jnp.float32), axis=2)
    grad_weights = jnp.einsum(
        "rgd,jwd->jgrw", cotangent_heads, value_blocks, preferred_element_type=jnp.float32
    )
    grad_scores = (weights * (grad_weights - row_delta.T[None, :, :, None])).astype(jnp.bfloat16)
    query_term = jnp.einsum(
        "jgrw,jwd->rgd", grad_scores, key_blocks, preferred_element_type=jnp.float32
    )
    key_term = jnp.einsum(
        "jgrw,rgd->jwd", grad_scores, query_heads, preferred_element_type=jnp.float32
    )
    value_term = jnp.einsum(
        "jgrw,rgd->jwd", weights_low, cotangent_heads, preferred_element_type=jnp.float32
    )
    grad_query = (softmax_scale * query_term).astype(jnp.bfloat16)
    return (out_low, grad_query, softmax_scale * key_term, value_term)


def block_mask(doc_ids, seg_pad, block_index, row_start, query_count, row_count, block_span):
    window = block_span * row_count
    padding = (block_span - 1) * row_count
    base_row = block_index * row_count
    seg_query = lax.dynamic_slice_in_dim(doc_ids, base_row + row_start, query_count, 0)
    seg_keys = lax.dynamic_slice_in_dim(seg_pad, base_row, window, 0)
    query_pos = base_row + row_start + jnp.arange(query_count, dtype=jnp.int32)
    key_pos = base_row - padding + jnp.arange(window, dtype=jnp.int32)
    allowed = (seg_query[:, None] == seg_keys[None, :]) & (key_pos[None, :] <= query_pos[:, None])
    allowed_blocks = jnp.transpose(allowed.reshape(query_count, block_span, row_count), (1, 0, 2))
    live_blocks = jnp.any(allowed_blocks, axis=(1, 2))
    return (allowed_blocks, live_blocks)


def run_heads(query_rows, cotangent_rows, key_window, value_window, allowed_blocks):
    query_count = query_rows.shape[0]
    block_span = key_window.shape[0]
    key_rows = key_window.shape[1]
    kv_columns = key_window.shape[2]
    local_kv = kv_columns // HEAD_DIM
    group_size = QHEADS // KVHEADS

    def head_step(head_index, state):
        out_buffer, dq_buffer, key_terms, value_terms = state
        column = head_index * group_size * HEAD_DIM
        query_heads = lax.dynamic_slice_in_dim(
            query_rows, column, group_size * HEAD_DIM, 1
        ).reshape(query_count, group_size, HEAD_DIM)
        cotangent_heads = lax.dynamic_slice_in_dim(
            cotangent_rows, column, group_size * HEAD_DIM, 1
        ).reshape(query_count, group_size, HEAD_DIM)
        key_blocks = lax.dynamic_slice_in_dim(key_window, head_index * HEAD_DIM, HEAD_DIM, 2)
        value_blocks = lax.dynamic_slice_in_dim(value_window, head_index * HEAD_DIM, HEAD_DIM, 2)
        out_heads, grad_query, key_term, value_term = attend(
            query_heads, cotangent_heads, key_blocks, value_blocks, allowed_blocks
        )
        out_buffer = lax.dynamic_update_slice_in_dim(
            out_buffer, out_heads.reshape(query_count, group_size * HEAD_DIM), column, 1
        )
        dq_buffer = lax.dynamic_update_slice_in_dim(
            dq_buffer, grad_query.reshape(query_count, group_size * HEAD_DIM), column, 1
        )
        key_terms = lax.dynamic_update_slice_in_dim(key_terms, key_term, head_index * HEAD_DIM, 2)
        value_terms = lax.dynamic_update_slice_in_dim(
            value_terms, value_term, head_index * HEAD_DIM, 2
        )
        return (out_buffer, dq_buffer, key_terms, value_terms)

    start_state = (
        jnp.zeros(query_rows.shape, jnp.bfloat16),
        jnp.zeros(query_rows.shape, jnp.bfloat16),
        jnp.zeros((block_span, key_rows, kv_columns), jnp.float32),
        jnp.zeros((block_span, key_rows, kv_columns), jnp.float32),
    )
    return lax.fori_loop(0, local_kv, head_step, start_state)


def body(queries, keys, values, grad_out, segments):
    row_count = queries.shape[0]
    block_span = DEPTH + 1
    padding = DEPTH * row_count
    my_index = lax.axis_index("dp")
    seg_pad = jnp.concatenate([jnp.full((padding,), -1, jnp.int32), segments])
    grad_heads = lax.all_to_all(grad_out, "head", split_axis=1, concat_axis=0, tiled=True)
    key_parts = []
    value_parts = []
    for distance in range(DEPTH, 0, -1):
        moved_key, moved_value = from_behind((keys, values), "dp", distance)
        key_parts.append(moved_key)
        value_parts.append(moved_value)
    key_parts.append(keys)
    value_parts.append(values)
    key_window = jnp.stack(key_parts)
    value_window = jnp.stack(value_parts)
    allowed_blocks, live_blocks = block_mask(
        segments, seg_pad, my_index, 0, row_count, row_count, block_span
    )
    out_buffer, grad_queries, key_terms, value_terms = run_heads(
        queries, grad_heads, key_window, value_window, allowed_blocks
    )
    summed_key = key_terms[DEPTH]
    summed_value = value_terms[DEPTH]
    for distance in range(1, DEPTH + 1):
        moved_key, moved_value = from_behind(
            (key_terms[DEPTH - distance], value_terms[DEPTH - distance]), "dp", -distance
        )
        summed_key = summed_key + moved_key
        summed_value = summed_value + moved_value
    attention_out = lax.all_to_all(out_buffer, "head", split_axis=0, concat_axis=1, tiled=True)
    return (
        attention_out,
        grad_queries,
        summed_key.astype(jnp.bfloat16),
        summed_value.astype(jnp.bfloat16),
    )


def solution(mesh):
    placed = (P("dp", "head"), P("dp", "head"), P("dp", "head"), P(("dp", "head"), None), P())
    return jax.shard_map(
        body,
        mesh=mesh,
        in_specs=placed,
        out_specs=(P(("dp", "head"), None), P("dp", "head"), P("dp", "head"), P("dp", "head")),
        check_vma=False,
    )
```

profile of v0, /device:TPU:0, one launch (start us, length us, event | category | flops | bytes accessed | tf_op | source)
XLA Modules:
  0.0 378.5 jit_solution(6137696104916197373)
XLA Ops:
  1.7 4.8 %collective-permute-start.7 = (bf16[128,512]{0,1:T(8,128)(2,1)S(1)}, bf16[128,512]{0,1:T(8,128)(2,1)S(1)}, u32[]{:S(2)}, u32[]{:S(2)}) collective-permute-start(bf16[128,512]{0,1:T(8,128)(2,1)S(1)} %copy.79), channel_id=1, source_target_pairs={{0,2},{2,4},{4,6},{6,8},{8,10},{10,12},{12,14},{14,16},{16,18},{18... | collective-permute-start | bytes 393224 | tf_op jit(solution)/shard_map/ppermute | solution.py:17
  6.5 3.4 collective-permute-start.6
  10.0 4.4 %collective-permute-start.5 = (bf16[128,512]{0,1:T(8,128)(2,1)S(1)}, bf16[128,512]{0,1:T(8,128)(2,1)S(1)}, u32[]{:S(2)}, u32[]{:S(2)}) collective-permute-start(bf16[128,512]{0,1:T(8,128)(2,1)S(1)} %copy.79), channel_id=1, source_target_pairs={{0,6},{2,8},{4,10},{6,12},{8,14},{10,16},{12,18},{14,20},{16,22},{... | collective-permute-start | bytes 393224 | tf_op jit(solution)/shard_map/ppermute | solution.py:17
  14.3 3.5 collective-permute-start.4
  17.8 2.9 collective-permute-start.8
  23.4 4.8 %all-to-all-start = ((bf16[64,2,6144]{2,0,1:T(8,128)(2,1)}), bf16[64,2,6144]{2,0,1:T(8,128)(2,1)}, u32[]{:S(2)}, u32[]{:S(2)}) async-start(bf16[64,2,6144]{2,0,1:T(8,128)(2,1)} %bitcast.207), calls=%async_computation | async-start | bytes 3145728 | tf_op jit(solution)/shard_map/all_to_all | solution.py:117
  30.4 2.9 collective-permute-done.9
  33.4 5.5 %collective-permute-start.10 = (bf16[128,512]{1,0:T(8,128)(2,1)S(1)}, bf16[128,512]{1,0:T(8,128)(2,1)S(1)}, u32[]{:S(2)}, u32[]{:S(2)}) collective-permute-start(bf16[128,512]{1,0:T(8,128)(2,1)S(1)} %copy-done.7), channel_id=1, source_target_pairs={{0,12},{2,14},{4,16},{6,18},{8,20},{10,22},{12,24},{14,26},{16,28}... | collective-permute-start | bytes 393224 | tf_op jit(solution)/shard_map/ppermute | solution.py:17
  46.6 7.4 %collective-permute-start.12 = (bf16[128,512]{1,0:T(8,128)(2,1)S(1)}, bf16[128,512]{1,0:T(8,128)(2,1)S(1)}, u32[]{:S(2)}, u32[]{:S(2)}) collective-permute-start(bf16[128,512]{1,0:T(8,128)(2,1)S(1)} %copy-done.7), channel_id=1, source_target_pairs={{0,8},{2,10},{4,12},{6,14},{8,16},{10,18},{12,20},{14,22},{16,24},... | collective-permute-start | bytes 393224 | tf_op jit(solution)/shard_map/ppermute | solution.py:17
  56.5 6.8 %collective-permute-start.13 = (bf16[128,512]{1,0:T(8,128)(2,1)S(1)}, bf16[128,512]{1,0:T(8,128)(2,1)S(1)}, u32[]{:S(2)}, u32[]{:S(2)}) collective-permute-start(bf16[128,512]{1,0:T(8,128)(2,1)S(1)} %copy-done.7), channel_id=1, source_target_pairs={{0,6},{2,8},{4,10},{6,12},{8,14},{10,16},{12,18},{14,20},{16,22},{... | collective-permute-start | bytes 393224 | tf_op jit(solution)/shard_map/ppermute | solution.py:17
  70.1 6.0 %collective-permute-start.15 = (bf16[128,512]{1,0:T(8,128)(2,1)S(1)}, bf16[128,512]{1,0:T(8,128)(2,1)S(1)}, u32[]{:S(2)}, u32[]{:S(2)}) collective-permute-start(bf16[128,512]{1,0:T(8,128)(2,1)S(1)} %copy-done.7), channel_id=1, source_target_pairs={{0,2},{2,4},{4,6},{6,8},{8,10},{10,12},{12,14},{14,16},{16,18},{18... | collective-permute-start | bytes 393224 | tf_op jit(solution)/shard_map/ppermute | solution.py:17
  78.6 12.2 %collective-permute-start = (bf16[128,512]{0,1:T(8,128)(2,1)S(1)}, bf16[128,512]{0,1:T(8,128)(2,1)S(1)}, u32[]{:S(2)}, u32[]{:S(2)}) collective-permute-start(bf16[128,512]{0,1:T(8,128)(2,1)S(1)} %copy.79), channel_id=1, source_target_pairs={{0,16},{2,18},{4,20},{6,22},{8,24},{10,26},{12,28},{14,30},{1,17},... | collective-permute-start | bytes 393224 | tf_op jit(solution)/shard_map/ppermute | solution.py:17
  96.4 2.9 collective-permute-done.1
  99.3 9.3 %collective-permute-start.2 = (bf16[128,512]{0,1:T(8,128)(2,1)S(1)}, bf16[128,512]{0,1:T(8,128)(2,1)S(1)}, u32[]{:S(2)}, u32[]{:S(2)}) collective-permute-start(bf16[128,512]{0,1:T(8,128)(2,1)S(1)} %copy.79), channel_id=1, source_target_pairs={{0,12},{2,14},{4,16},{6,18},{8,20},{10,22},{12,24},{14,26},{16,28}... | collective-permute-start | bytes 393224 | tf_op jit(solution)/shard_map/ppermute | solution.py:17
  125.0 112.0 %while.22 = (s32[]{:T(128)}, bf16[128,6144]{1,0:T(8,128)(2,1)}, bf16[128,6144]{1,0:T(8,128)(2,1)}, f32[9,128,512]{2,1,0:T(8,128)}, f32[9,128,512]{2,1,0:T(8,128)...) while((s32[]{:T(128)}, bf16[128,6144]{1,0:T(8,128)(2,1)}, ...), condition=%wide.region_4.5_spmd.clone, body=%wide.region_0.4_spmd.clone.sunk | while | flops 2757030912 | bytes 114602480 | solution.py:108
  133.6 2.9 fusion.84
  139.5 5.6 %fusion.88 = f32[9,128,512]{2,1,0:T(8,128)} fusion(f32[9,128,512]{2,1,0:T(8,128)} %get-tuple-element.496, s32[]{:T(128)S(6)} %select_n.72, bf16[128,12,128,1]{0,2,1,3:T(8,128)(2,1)} %bitcast.267, f32[9,128,128,12]{2,1,3,0:T(8,128)} %copy-done, f32[12,128]{1,0:T(8,128)S(1)} %log_add_fusion.2, pred[9,128,128]{1,2,0:T(8,128)(4,1)S(1)} %compare_and_fusion.2), kind=kOutput, calls=%fused_computation.13.clone.1 | convolution fusion | flops 460062720 | bytes 8214532 | tf_op jit(solution)/shard_map/while/body/eval_jaxpr/jgrw,rgd->jwd/dot_general | solution.py:47
  145.1 3.2 fusion.85
  167.5 5.6 %fusion.88 = f32[9,128,512]{2,1,0:T(8,128)} fusion(f32[9,128,512]{2,1,0:T(8,128)} %get-tuple-element.496, s32[]{:T(128)S(6)} %select_n.72, bf16[128,12,128,1]{0,2,1,3:T(8,128)(2,1)} %bitcast.267, f32[9,128,128,12]{2,1,3,0:T(8,128)} %copy-done, f32[12,128]{1,0:T(8,128)S(1)} %log_add_fusion.2, pred[9,128,128]{1,2,0:T(8,128)(4,1)S(1)} %compare_and_fusion.2), kind=kOutput, calls=%fused_computation.13.clone.1 | convolution fusion | flops 460062720 | bytes 8214532 | tf_op jit(solution)/shard_map/while/body/eval_jaxpr/jgrw,rgd->jwd/dot_general | solution.py:47
  173.1 3.2 fusion.85
  189.7 2.9 fusion.84
  195.5 5.6 %fusion.88 = f32[9,128,512]{2,1,0:T(8,128)} fusion(f32[9,128,512]{2,1,0:T(8,128)} %get-tuple-element.496, s32[]{:T(128)S(6)} %select_n.72, bf16[128,12,128,1]{0,2,1,3:T(8,128)(2,1)} %bitcast.267, f32[9,128,128,12]{2,1,3,0:T(8,128)} %copy-done, f32[12,128]{1,0:T(8,128)S(1)} %log_add_fusion.2, pred[9,128,128]{1,2,0:T(8,128)(4,1)S(1)} %compare_and_fusion.2), kind=kOutput, calls=%fused_computation.13.clone.1 | convolution fusion | flops 460062720 | bytes 8214532 | tf_op jit(solution)/shard_map/while/body/eval_jaxpr/jgrw,rgd->jwd/dot_general | solution.py:47
  201.1 3.1 fusion.85
  217.7 2.9 fusion.84
  223.5 5.6 %fusion.88 = f32[9,128,512]{2,1,0:T(8,128)} fusion(f32[9,128,512]{2,1,0:T(8,128)} %get-tuple-element.496, s32[]{:T(128)S(6)} %select_n.72, bf16[128,12,128,1]{0,2,1,3:T(8,128)(2,1)} %bitcast.267, f32[9,128,128,12]{2,1,3,0:T(8,128)} %copy-done, f32[12,128]{1,0:T(8,128)S(1)} %log_add_fusion.2, pred[9,128,128]{1,2,0:T(8,128)(4,1)S(1)} %compare_and_fusion.2), kind=kOutput, calls=%fused_computation.13.clone.1 | convolution fusion | flops 460062720 | bytes 8214532 | tf_op jit(solution)/shard_map/while/body/eval_jaxpr/jgrw,rgd->jwd/dot_general | solution.py:47
  229.1 3.1 fusion.85
  245.4 8.7 %collective-permute-done.24 = f32[128,512]{1,0:T(8,128)S(1)} collective-permute-done((f32[128,512]{1,0:T(8,128)S(1)}, f32[128,512]{1,0:T(8,128)S(1)}, u32[]{:S(2)}, u32[]{:S(2)}) %collective-permute-start.24) | collective-permute-done | bytes 262176 | tf_op jit(solution)/shard_map/ppermute | solution.py:17
  255.7 4.4 %collective-permute-done.30 = f32[128,512]{1,0:T(8,128)S(1)} collective-permute-done((f32[128,512]{1,0:T(8,128)S(1)}, f32[128,512]{1,0:T(8,128)S(1)}, u32[]{:S(2)}, u32[]{:S(2)}) %collective-permute-start.30) | collective-permute-done | bytes 262176 | tf_op jit(solution)/shard_map/ppermute | solution.py:17
  271.3 5.0 %all_to_all.38 = bf16[2,64,6144]{2,1,0:T(8,128)(2,1)S(1)} all-to-all(bf16[2,64,6144]{2,1,0:T(8,128)(2,1)S(1)} %bitcast.271), channel_id=1, replica_groups=mesh['dp'=16,'head'=2] {'head'}, dimensions={0} | all-to-all | bytes 3145728 | tf_op jit(solution)/shard_map/all_to_all | solution.py:142
  278.9 53.6 %collective-permute-done.31 = f32[128,512]{1,0:T(8,128)S(1)} collective-permute-done((f32[128,512]{1,0:T(8,128)S(1)}, f32[128,512]{1,0:T(8,128)S(1)}, u32[]{:S(2)}, u32[]{:S(2)}) %collective-permute-start.31) | collective-permute-done | bytes 262176 | tf_op jit(solution)/shard_map/ppermute | solution.py:17
  339.5 7.6 %collective-permute-done.19 = f32[128,512]{1,0:T(8,128)S(1)} collective-permute-done((f32[128,512]{1,0:T(8,128)S(1)}, f32[128,512]{1,0:T(8,128)S(1)}, u32[]{:S(2)}, u32[]{:S(2)}) %collective-permute-start.19) | collective-permute-done | bytes 262176 | tf_op jit(solution)/shard_map/ppermute | solution.py:17
  347.2 30.5 %collective-permute-done.23 = f32[128,512]{1,0:T(8,128)S(1)} collective-permute-done((f32[128,512]{1,0:T(8,128)S(1)}, f32[128,512]{1,0:T(8,128)S(1)}, u32[]{:S(2)}, u32[]{:S(2)}) %collective-permute-start.23) | collective-permute-done | bytes 262176 | tf_op jit(solution)/shard_map/ppermute | solution.py:17
  (205 shorter events, 146.6 us)
Async XLA Ops:
  1.7 116.0 %collective-permute-start.7 = (bf16[128,512]{0,1:T(8,128)(2,1)S(1)}, bf16[128,512]{0,1:T(8,128)(2,1)S(1)}, u32[]{:S(2)}, u32[]{:S(2)}) collective-permute-start(bf16[128,512]{0,1:T(8,128)(2,1)S(1)} %copy.79), channel_id=1, source_target_pairs={{0,2},{2,4},{4,6},{6,8},{8,10},{10,12},{12,14},{14,16},{16,18},{18... | collective-permute-start | bytes 393224 | tf_op jit(solution)/shard_map/ppermute | solution.py:17
  6.5 110.5 %collective-permute-start.6 = (bf16[128,512]{0,1:T(8,128)(2,1)S(1)}, bf16[128,512]{0,1:T(8,128)(2,1)S(1)}, u32[]{:S(2)}, u32[]{:S(2)}) collective-permute-start(bf16[128,512]{0,1:T(8,128)(2,1)S(1)} %copy.79), channel_id=1, source_target_pairs={{0,4},{2,6},{4,8},{6,10},{8,12},{10,14},{12,16},{14,18},{16,20},{1... | collective-permute-start | bytes 393224 | tf_op jit(solution)/shard_map/ppermute | solution.py:17
  10.0 106.4 %collective-permute-start.5 = (bf16[128,512]{0,1:T(8,128)(2,1)S(1)}, bf16[128,512]{0,1:T(8,128)(2,1)S(1)}, u32[]{:S(2)}, u32[]{:S(2)}) collective-permute-start(bf16[128,512]{0,1:T(8,128)(2,1)S(1)} %copy.79), channel_id=1, source_target_pairs={{0,6},{2,8},{4,10},{6,12},{8,14},{10,16},{12,18},{14,20},{16,22},{... | collective-permute-start | bytes 393224 | tf_op jit(solution)/shard_map/ppermute | solution.py:17
  14.3 101.4 %collective-permute-start.4 = (bf16[128,512]{0,1:T(8,128)(2,1)S(1)}, bf16[128,512]{0,1:T(8,128)(2,1)S(1)}, u32[]{:S(2)}, u32[]{:S(2)}) collective-permute-start(bf16[128,512]{0,1:T(8,128)(2,1)S(1)} %copy.79), channel_id=1, source_target_pairs={{0,8},{2,10},{4,12},{6,14},{8,16},{10,18},{12,20},{14,22},{16,24},... | collective-permute-start | bytes 393224 | tf_op jit(solution)/shard_map/ppermute | solution.py:17
  17.8 10.6 %collective-permute-start.8 = (bf16[128,512]{1,0:T(8,128)(2,1)}, bf16[128,512]{1,0:T(8,128)(2,1)S(1)}, u32[]{:S(2)}, u32[]{:S(2)}) collective-permute-start(bf16[128,512]{1,0:T(8,128)(2,1)} %param.8), channel_id=1, source_target_pairs={{0,16},{2,18},{4,20},{6,22},{8,24},{10,26},{12,28},{14,30},{1,17},... | collective-permute-start | bytes 393224 | tf_op jit(solution)/shard_map/ppermute | solution.py:17
  23.4 95.6 %all-to-all-start = ((bf16[64,2,6144]{2,0,1:T(8,128)(2,1)}), bf16[64,2,6144]{2,0,1:T(8,128)(2,1)}, u32[]{:S(2)}, u32[]{:S(2)}) async-start(bf16[64,2,6144]{2,0,1:T(8,128)(2,1)} %bitcast.207), calls=%async_computation | async-start | bytes 3145728 | tf_op jit(solution)/shard_map/all_to_all | solution.py:117
  28.4 5.0 %collective-permute-start.9 = (bf16[128,512]{1,0:T(8,128)(2,1)S(1)}, bf16[128,512]{1,0:T(8,128)(2,1)S(1)}, u32[]{:S(2)}, u32[]{:S(2)}) collective-permute-start(bf16[128,512]{1,0:T(8,128)(2,1)S(1)} %copy-done.7), channel_id=1, source_target_pairs={{0,14},{2,16},{4,18},{6,20},{8,22},{10,24},{12,26},{14,28},{16,30}... | collective-permute-start | bytes 393224 | tf_op jit(solution)/shard_map/ppermute | solution.py:17
  33.4 8.0 %collective-permute-start.10 = (bf16[128,512]{1,0:T(8,128)(2,1)S(1)}, bf16[128,512]{1,0:T(8,128)(2,1)S(1)}, u32[]{:S(2)}, u32[]{:S(2)}) collective-permute-start(bf16[128,512]{1,0:T(8,128)(2,1)S(1)} %copy-done.7), channel_id=1, source_target_pairs={{0,12},{2,14},{4,16},{6,18},{8,20},{10,22},{12,24},{14,26},{16,28}... | collective-permute-start | bytes 393224 | tf_op jit(solution)/shard_map/ppermute | solution.py:17
  41.4 5.2 %collective-permute-start.11 = (bf16[128,512]{1,0:T(8,128)(2,1)S(1)}, bf16[128,512]{1,0:T(8,128)(2,1)S(1)}, u32[]{:S(2)}, u32[]{:S(2)}) collective-permute-start(bf16[128,512]{1,0:T(8,128)(2,1)S(1)} %copy-done.7), channel_id=1, source_target_pairs={{0,10},{2,12},{4,14},{6,16},{8,18},{10,20},{12,22},{14,24},{16,26}... | collective-permute-start | bytes 393224 | tf_op jit(solution)/shard_map/ppermute | solution.py:17
  46.6 9.9 %collective-permute-start.12 = (bf16[128,512]{1,0:T(8,128)(2,1)S(1)}, bf16[128,512]{1,0:T(8,128)(2,1)S(1)}, u32[]{:S(2)}, u32[]{:S(2)}) collective-permute-start(bf16[128,512]{1,0:T(8,128)(2,1)S(1)} %copy-done.7), channel_id=1, source_target_pairs={{0,8},{2,10},{4,12},{6,14},{8,16},{10,18},{12,20},{14,22},{16,24},... | collective-permute-start | bytes 393224 | tf_op jit(solution)/shard_map/ppermute | solution.py:17
  56.5 9.3 %collective-permute-start.13 = (bf16[128,512]{1,0:T(8,128)(2,1)S(1)}, bf16[128,512]{1,0:T(8,128)(2,1)S(1)}, u32[]{:S(2)}, u32[]{:S(2)}) collective-permute-start(bf16[128,512]{1,0:T(8,128)(2,1)S(1)} %copy-done.7), channel_id=1, source_target_pairs={{0,6},{2,8},{4,10},{6,12},{8,14},{10,16},{12,18},{14,20},{16,22},{... | collective-permute-start | bytes 393224 | tf_op jit(solution)/shard_map/ppermute | solution.py:17
  65.8 4.3 %collective-permute-start.14 = (bf16[128,512]{1,0:T(8,128)(2,1)S(1)}, bf16[128,512]{1,0:T(8,128)(2,1)S(1)}, u32[]{:S(2)}, u32[]{:S(2)}) collective-permute-start(bf16[128,512]{1,0:T(8,128)(2,1)S(1)} %copy-done.7), channel_id=1, source_target_pairs={{0,4},{2,6},{4,8},{6,10},{8,12},{10,14},{12,16},{14,18},{16,20},{1... | collective-permute-start | bytes 393224 | tf_op jit(solution)/shard_map/ppermute | solution.py:17
  70.1 8.5 %collective-permute-start.15 = (bf16[128,512]{1,0:T(8,128)(2,1)S(1)}, bf16[128,512]{1,0:T(8,128)(2,1)S(1)}, u32[]{:S(2)}, u32[]{:S(2)}) collective-permute-start(bf16[128,512]{1,0:T(8,128)(2,1)S(1)} %copy-done.7), channel_id=1, source_target_pairs={{0,2},{2,4},{4,6},{6,8},{8,10},{10,12},{12,14},{14,16},{16,18},{18... | collective-permute-start | bytes 393224 | tf_op jit(solution)/shard_map/ppermute | solution.py:17
  78.6 14.7 %collective-permute-start = (bf16[128,512]{0,1:T(8,128)(2,1)S(1)}, bf16[128,512]{0,1:T(8,128)(2,1)S(1)}, u32[]{:S(2)}, u32[]{:S(2)}) collective-permute-start(bf16[128,512]{0,1:T(8,128)(2,1)S(1)} %copy.79), channel_id=1, source_target_pairs={{0,16},{2,18},{4,20},{6,22},{8,24},{10,26},{12,28},{14,30},{1,17},... | collective-permute-start | bytes 393224 | tf_op jit(solution)/shard_map/ppermute | solution.py:17
  93.3 6.0 %collective-permute-start.1 = (bf16[128,512]{0,1:T(8,128)(2,1)S(1)}, bf16[128,512]{0,1:T(8,128)(2,1)S(1)}, u32[]{:S(2)}, u32[]{:S(2)}) collective-permute-start(bf16[128,512]{0,1:T(8,128)(2,1)S(1)} %copy.79), channel_id=1, source_target_pairs={{0,14},{2,16},{4,18},{6,20},{8,22},{10,24},{12,26},{14,28},{16,30}... | collective-permute-start | bytes 393224 | tf_op jit(solution)/shard_map/ppermute | solution.py:17
  99.3 12.0 %collective-permute-start.2 = (bf16[128,512]{0,1:T(8,128)(2,1)S(1)}, bf16[128,512]{0,1:T(8,128)(2,1)S(1)}, u32[]{:S(2)}, u32[]{:S(2)}) collective-permute-start(bf16[128,512]{0,1:T(8,128)(2,1)S(1)} %copy.79), channel_id=1, source_target_pairs={{0,12},{2,14},{4,16},{6,18},{8,20},{10,22},{12,24},{14,26},{16,28}... | collective-permute-start | bytes 393224 | tf_op jit(solution)/shard_map/ppermute | solution.py:17
  238.9 15.2 %collective-permute-start.24 = (f32[128,512]{1,0:T(8,128)S(1)}, f32[128,512]{1,0:T(8,128)S(1)}, u32[]{:S(2)}, u32[]{:S(2)}) collective-permute-start(f32[128,512]{1,0:T(8,128)S(1)} %get-tuple-element.370), channel_id=1, source_target_pairs={{2,0},{4,2},{6,4},{8,6},{10,8},{12,10},{14,12},{16,14},{18,16},{20... | collective-permute-start | bytes 786440 | tf_op jit(solution)/shard_map/ppermute | solution.py:17
  240.2 19.8 %collective-permute-start.30 = (f32[128,512]{1,0:T(8,128)S(1)}, f32[128,512]{1,0:T(8,128)S(1)}, u32[]{:S(2)}, u32[]{:S(2)}) collective-permute-start(f32[128,512]{1,0:T(8,128)S(1)} %get-tuple-element.371), channel_id=1, source_target_pairs={{14,0},{16,2},{18,4},{20,6},{22,8},{24,10},{26,12},{28,14},{30,16}... | collective-permute-start | bytes 786440 | tf_op jit(solution)/shard_map/ppermute | solution.py:17
  241.5 21.5 %collective-permute-start.29 = (f32[128,512]{1,0:T(8,128)S(1)}, f32[128,512]{1,0:T(8,128)S(1)}, u32[]{:S(2)}, u32[]{:S(2)}) collective-permute-start(f32[128,512]{1,0:T(8,128)S(1)} %get-tuple-element.372), channel_id=1, source_target_pairs={{12,0},{14,2},{16,4},{18,6},{20,8},{22,10},{24,12},{26,14},{28,16}... | collective-permute-start | bytes 786440 | tf_op jit(solution)/shard_map/ppermute | solution.py:17
  242.8 21.4 %collective-permute-start.28 = (f32[128,512]{1,0:T(8,128)S(1)}, f32[128,512]{1,0:T(8,128)S(1)}, u32[]{:S(2)}, u32[]{:S(2)}) collective-permute-start(f32[128,512]{1,0:T(8,128)S(1)} %get-tuple-element.373), channel_id=1, source_target_pairs={{10,0},{12,2},{14,4},{16,6},{18,8},{20,10},{22,12},{24,14},{26,16}... | collective-permute-start | bytes 786440 | tf_op jit(solution)/shard_map/ppermute | solution.py:17
  244.1 21.9 %collective-permute-start.27 = (f32[128,512]{1,0:T(8,128)S(1)}, f32[128,512]{1,0:T(8,128)S(1)}, u32[]{:S(2)}, u32[]{:S(2)}) collective-permute-start(f32[128,512]{1,0:T(8,128)S(1)} %get-tuple-element.374), channel_id=1, source_target_pairs={{8,0},{10,2},{12,4},{14,6},{16,8},{18,10},{20,12},{22,14},{24,16},... | collective-permute-start | bytes 786440 | tf_op jit(solution)/shard_map/ppermute | solution.py:17
  254.2 15.8 %collective-permute-start.26 = (f32[128,512]{1,0:T(8,128)S(1)}, f32[128,512]{1,0:T(8,128)S(1)}, u32[]{:S(2)}, u32[]{:S(2)}) collective-permute-start(f32[128,512]{1,0:T(8,128)S(1)} %get-tuple-element.375), channel_id=1, source_target_pairs={{6,0},{8,2},{10,4},{12,6},{14,8},{16,10},{18,12},{20,14},{22,16},{... | collective-permute-start | bytes 786440 | tf_op jit(solution)/shard_map/ppermute | solution.py:17
  260.0 17.5 %collective-permute-start.25 = (f32[128,512]{1,0:T(8,128)S(1)}, f32[128,512]{1,0:T(8,128)S(1)}, u32[]{:S(2)}, u32[]{:S(2)}) collective-permute-start(f32[128,512]{1,0:T(8,128)S(1)} %get-tuple-element.376), channel_id=1, source_target_pairs={{4,0},{6,2},{8,4},{10,6},{12,8},{14,10},{16,12},{18,14},{20,16},{2... | collective-permute-start | bytes 786440 | tf_op jit(solution)/shard_map/ppermute | solution.py:17
  263.0 69.5 %collective-permute-start.31 = (f32[128,512]{1,0:T(8,128)S(1)}, f32[128,512]{1,0:T(8,128)S(1)}, u32[]{:S(2)}, u32[]{:S(2)}) collective-permute-start(f32[128,512]{1,0:T(8,128)S(1)} %get-tuple-element.377), channel_id=1, source_target_pairs={{16,0},{18,2},{20,4},{22,6},{24,8},{26,10},{28,12},{30,14},{17,1},... | collective-permute-start | bytes 786440 | tf_op jit(solution)/shard_map/ppermute | solution.py:17
  264.3 69.5 %collective-permute-start.16 = (f32[128,512]{1,0:T(8,128)S(1)}, f32[128,512]{1,0:T(8,128)S(1)}, u32[]{:S(2)}, u32[]{:S(2)}) collective-permute-start(f32[128,512]{1,0:T(8,128)S(1)} %get-tuple-element.378), channel_id=1, source_target_pairs={{2,0},{4,2},{6,4},{8,6},{10,8},{12,10},{14,12},{16,14},{18,16},{20... | collective-permute-start | bytes 786440 | tf_op jit(solution)/shard_map/ppermute | solution.py:17
  266.1 69.0 %collective-permute-start.22 = (f32[128,512]{1,0:T(8,128)S(1)}, f32[128,512]{1,0:T(8,128)S(1)}, u32[]{:S(2)}, u32[]{:S(2)}) collective-permute-start(f32[128,512]{1,0:T(8,128)S(1)} %get-tuple-element.379), channel_id=1, source_target_pairs={{14,0},{16,2},{18,4},{20,6},{22,8},{24,10},{26,12},{28,14},{30,16}... | collective-permute-start | bytes 786440 | tf_op jit(solution)/shard_map/ppermute | solution.py:17
  270.0 66.4 %collective-permute-start.21 = (f32[128,512]{1,0:T(8,128)S(1)}, f32[128,512]{1,0:T(8,128)S(1)}, u32[]{:S(2)}, u32[]{:S(2)}) collective-permute-start(f32[128,512]{1,0:T(8,128)S(1)} %get-tuple-element.380), channel_id=1, source_target_pairs={{12,0},{14,2},{16,4},{18,6},{20,8},{22,10},{24,12},{26,14},{28,16}... | collective-permute-start | bytes 786440 | tf_op jit(solution)/shard_map/ppermute | solution.py:17
  277.6 61.9 %collective-permute-start.20 = (f32[128,512]{1,0:T(8,128)S(1)}, f32[128,512]{1,0:T(8,128)S(1)}, u32[]{:S(2)}, u32[]{:S(2)}) collective-permute-start(f32[128,512]{1,0:T(8,128)S(1)} %get-tuple-element.381), channel_id=1, source_target_pairs={{10,0},{12,2},{14,4},{16,6},{18,8},{20,10},{22,12},{24,14},{26,16}... | collective-permute-start | bytes 786440 | tf_op jit(solution)/shard_map/ppermute | solution.py:17
  332.5 14.7 %collective-permute-start.19 = (f32[128,512]{1,0:T(8,128)S(1)}, f32[128,512]{1,0:T(8,128)S(1)}, u32[]{:S(2)}, u32[]{:S(2)}) collective-permute-start(f32[128,512]{1,0:T(8,128)S(1)} %get-tuple-element.382), channel_id=1, source_target_pairs={{8,0},{10,2},{12,4},{14,6},{16,8},{18,10},{20,12},{22,14},{24,16},... | collective-permute-start | bytes 786440 | tf_op jit(solution)/shard_map/ppermute | solution.py:17
  333.8 13.4 %collective-permute-start.18 = (f32[128,512]{1,0:T(8,128)S(1)}, f32[128,512]{1,0:T(8,128)S(1)}, u32[]{:S(2)}, u32[]{:S(2)}) collective-permute-start(f32[128,512]{1,0:T(8,128)S(1)} %get-tuple-element.383), channel_id=1, source_target_pairs={{6,0},{8,2},{10,4},{12,6},{14,8},{16,10},{18,12},{20,14},{22,16},{... | collective-permute-start | bytes 786440 | tf_op jit(solution)/shard_map/ppermute | solution.py:17
  335.1 12.1 %collective-permute-start.17 = (f32[128,512]{1,0:T(8,128)S(1)}, f32[128,512]{1,0:T(8,128)S(1)}, u32[]{:S(2)}, u32[]{:S(2)}) collective-permute-start(f32[128,512]{1,0:T(8,128)S(1)} %get-tuple-element.384), channel_id=1, source_target_pairs={{4,0},{6,2},{8,4},{10,6},{12,8},{14,10},{16,12},{18,14},{20,16},{2... | collective-permute-start | bytes 786440 | tf_op jit(solution)/shard_map/ppermute | solution.py:17
  336.4 41.3 %collective-permute-start.23 = (f32[128,512]{1,0:T(8,128)S(1)}, f32[128,512]{1,0:T(8,128)S(1)}, u32[]{:S(2)}, u32[]{:S(2)}) collective-permute-start(f32[128,512]{1,0:T(8,128)S(1)} %get-tuple-element.385), channel_id=1, source_target_pairs={{16,0},{18,2},{20,4},{22,6},{24,8},{26,10},{28,12},{30,14},{17,1},... | collective-permute-start | bytes 786440 | tf_op jit(solution)/shard_map/ppermute | solution.py:17
  (33 other events, 161.2 us)
where the time goes:
time: 380 us; the launch traced here: 379 us
  waiting for transfers between devices  132 us (35%)
  starting transfers between devices  101 us (27%)
  matrix products  69.2 us (18%)
  local copies, waits for them, and re-layouts  59.2 us (16%)
  other arithmetic  10.8 us (3%)
  blocking collectives  5 us (1%)
    ppermute x32, waiting for transfers between devices, from_behind(): lax.ppermute(value, axis, [(source, source + steps) for source in range(f...  132 us
    ppermute x32, starting transfers between devices, from_behind(): lax.ppermute(value, axis, [(source, source + steps) for source in range(f...  96.4 us
    dot_general x4, matrix products, attend(): jnp.einsum('jgrw,rgd->jwd', weights_low, cotangent_heads, preferred_eleme...  22.3 us
    dot_general x4, matrix products, attend(): jnp.einsum('rgd,jwd->jgrw', cotangent_heads, value_blocks, preferred_elem...  12.6 us
    unnamed x25, local copies, waits for them, and re-layouts  11.6 us
    dot_general x4, matrix products, attend(): jnp.einsum('jgrw,jwd->rgd', weights_low, value_blocks, preferred_element_...  11.5 us
    dynamic_update_slice x4, local copies, waits for them, and re-layouts, head_step(): lax.dynamic_update_slice_in_dim(out_buffer, out_heads.reshape(query_count...  8.83 us
    dot_general x4, matrix products, attend(): jnp.einsum('rgd,jwd->jgrw', query_heads, key_blocks, preferred_element_ty...  8.16 us
  transfers between devices with their start and end apart: 33, of which 19 were waited for; matrix products, arithmetic and copies ran while one was open for 5% of the time, Pallas kernels for 0%

commit v1 on v0

v1 whole, which is shorter than its diff:
```python
import functools
import math

import jax
import jax.numpy as jnp
from jax import lax
from jax.experimental import pallas as pl
from jax.experimental.pallas import tpu as pltpu
from jax.sharding import PartitionSpec as P

QHEADS = 96
KVHEADS = 8
HEAD_DIM = 128
DEPTH = 8
SPAN = DEPTH + 1
GROUP = QHEADS // KVHEADS
PAIRS = GROUP // 2
MASKED = -(2.0**100)
SCALE = 1.0 / math.sqrt(HEAD_DIM)
NT = (((1,), (1,)), ((), ()))


def dot(a, b):
    return jnp.dot(a, b, preferred_element_type=jnp.float32)


def dot_nt(a, b):
    return lax.dot_general(a, b, NT, preferred_element_type=jnp.float32)


def attend_group(q_at, g_at, k_at, v_at, put_out, put_dq, put_dk, put_dv, tmp):
    (k_aug, v_aug, k_t, v_t, q_aug, g_aug, q_norm, g_norm, score, p_all, ds_all) = tmp
    rows = HEAD_DIM
    for j in range(SPAN):
        at = pl.ds(j * rows, rows)
        k_j, v_j = k_at(j), v_at(j)
        k_aug[at, :HEAD_DIM] = k_j
        v_aug[at, :HEAD_DIM] = v_j
        k_t[:, j * rows : (j + 1) * rows] = k_j.T
        v_t[:, j * rows : (j + 1) * rows] = v_j.T
    for h in range(GROUP):
        q_aug[h * rows : (h + 1) * rows, :HEAD_DIM] = q_at(h)
        g_aug[h * rows : (h + 1) * rows, :HEAD_DIM] = g_at(h)

    two = 2 * rows
    lane = lax.broadcasted_iota(jnp.int32, (two, HEAD_DIM), 1)

    def pair_step(pair, carry):
        cols = pl.ds(pl.multiple_of(pair * two, two), two)
        q_pair = q_aug[cols, :]
        score[...] = dot_nt(k_aug[...], q_pair)
        top = score[0:rows, :].reshape(rows // 8, 8, two).max(axis=0)
        for j in range(1, SPAN):
            part = score[j * rows : (j + 1) * rows, :]
            top = jnp.maximum(top, part.reshape(rows // 8, 8, two).max(axis=0))
        top = jnp.max(top, axis=0, keepdims=True)
        total = jnp.zeros((8, two), jnp.float32)
        for j in range(SPAN):
            part = score[j * rows : (j + 1) * rows, :]
            e = jnp.exp2((part - top) * (SCALE * math.log2(math.e)))
            total = total + e.reshape(rows // 8, 8, two).sum(axis=0)
            p_all[j * rows : (j + 1) * rows, cols] = e.astype(jnp.bfloat16)
        inv = 1.0 / jnp.sum(total, axis=0, keepdims=True)
        inv_t = jnp.broadcast_to(inv, (HEAD_DIM, two)).T
        p = p_all[:, cols]
        out = (dot(v_t[...], p).T * inv_t).astype(jnp.bfloat16)
        put_out(2 * pair, out[:rows])
        put_out(2 * pair + 1, out[rows:])
        g_pair = g_aug[cols, :HEAD_DIM].astype(jnp.float32)
        delta = -jnp.sum(g_pair * out.astype(jnp.float32), axis=1, keepdims=True)
        hi = delta.astype(jnp.bfloat16).astype(jnp.float32)
        mid = (delta - hi).astype(jnp.bfloat16).astype(jnp.float32)
        low = delta - hi - mid
        tail = jnp.where(lane == 0, hi, jnp.where(lane == 1, mid, jnp.where(lane == 2, low, 0.0)))
        g_aug[cols, HEAD_DIM:] = tail.astype(jnp.bfloat16)
        q_norm[cols, :] = (q_pair[:, :HEAD_DIM].astype(jnp.float32) * inv_t).astype(jnp.bfloat16)
        g_norm[cols, :] = (g_pair * inv_t).astype(jnp.bfloat16)
        score[...] = dot_nt(v_aug[...], g_aug[cols, :])
        for j in range(SPAN):
            at = slice(j * rows, (j + 1) * rows)
            ds_all[at, cols] = (p_all[at, cols].astype(jnp.float32) * score[at, :]).astype(jnp.bfloat16)
        dq = (dot(k_t[...], ds_all[:, cols]).T * (inv_t * SCALE)).astype(jnp.bfloat16)
        put_dq(2 * pair, dq[:rows])
        put_dq(2 * pair + 1, dq[rows:])
        return carry

    lax.fori_loop(0, PAIRS, pair_step, 0)
    for j in range(SPAN):
        at = slice(j * rows, (j + 1) * rows)
        put_dk(j, (SCALE * dot(ds_all[at, :], q_norm[...])).astype(jnp.bfloat16))
        put_dv(j, dot(p_all[at, :], g_norm[...]).astype(jnp.bfloat16))


def fill_constants(mask_ref, tmp):
    k_aug, v_aug, q_aug = tmp[0], tmp[1], tmp[4]
    k_aug[:, HEAD_DIM:] = mask_ref[...]
    ones = lax.broadcasted_iota(jnp.int32, (v_aug.shape[0], HEAD_DIM), 1) < 3
    v_aug[:, HEAD_DIM:] = jnp.where(ones, 1.0, 0.0).astype(jnp.bfloat16)
    side = (q_aug.shape[0], HEAD_DIM)
    row = lax.broadcasted_iota(jnp.int32, side, 0) % HEAD_DIM
    eye = row == lax.broadcasted_iota(jnp.int32, side, 1)
    q_aug[:, HEAD_DIM:] = jnp.where(eye, 1.0, 0.0).astype(jnp.bfloat16)


def scratch(rows):
    window, queries = SPAN * rows, GROUP * rows
    return [
        pltpu.VMEM((window, 2 * HEAD_DIM), jnp.bfloat16),
        pltpu.VMEM((window, 2 * HEAD_DIM), jnp.bfloat16),
        pltpu.VMEM((HEAD_DIM, window), jnp.bfloat16),
        pltpu.VMEM((HEAD_DIM, window), jnp.bfloat16),
        pltpu.VMEM((queries, 2 * HEAD_DIM), jnp.bfloat16),
        pltpu.VMEM((queries, 2 * HEAD_DIM), jnp.bfloat16),
        pltpu.VMEM((queries, HEAD_DIM), jnp.bfloat16),
        pltpu.VMEM((queries, HEAD_DIM), jnp.bfloat16),
        pltpu.VMEM((window, 2 * rows), jnp.float32),
        pltpu.VMEM((window, queries), jnp.bfloat16),
        pltpu.VMEM((window, queries), jnp.bfloat16),
    ]


def kernel(q_ref, g_ref, kv_ref, mask_ref, out_ref, dq_ref, dkv_ref, *tmp):
    @pl.when(pl.program_id(0) == 0)
    def _():
        fill_constants(mask_ref, tmp)

    def at(ref, h):
        return ref[:, h * HEAD_DIM : (h + 1) * HEAD_DIM]

    def put(ref, h, value):
        ref[:, pl.ds(pl.multiple_of(h * HEAD_DIM, HEAD_DIM), HEAD_DIM)] = value

    def put_block(which, j, value):
        dkv_ref[j, 0, which] = value

    attend_group(
        functools.partial(at, q_ref),
        functools.partial(at, g_ref),
        lambda j: kv_ref[j, 0, 0],
        lambda j: kv_ref[j, 0, 1],
        functools.partial(put, out_ref),
        functools.partial(put, dq_ref),
        functools.partial(put_block, 0),
        functools.partial(put_block, 1),
        tmp,
    )


def attention(queries, grad_heads, kv_window, mask):
    rows, columns = queries.shape
    heads = columns // (GROUP * HEAD_DIM)
    head_spec = pl.BlockSpec((rows, GROUP * HEAD_DIM), lambda h: (0, h))
    kv_spec = pl.BlockSpec((SPAN, 1, 2, rows, HEAD_DIM), lambda h: (0, h, 0, 0, 0))
    return pl.pallas_call(
        kernel,
        grid=(heads,),
        in_specs=[head_spec, head_spec, kv_spec, pl.BlockSpec(mask.shape, lambda h: (0, 0))],
        out_specs=[head_spec, head_spec, kv_spec],
        out_shape=[
            jax.ShapeDtypeStruct(queries.shape, jnp.bfloat16),
            jax.ShapeDtypeStruct(queries.shape, jnp.bfloat16),
            jax.ShapeDtypeStruct(kv_window.shape, jnp.bfloat16),
        ],
        scratch_shapes=scratch(rows),
        compiler_params=pltpu.CompilerParams(vmem_limit_bytes=48 * 1024 * 1024),
        name="attention",
    )(queries, grad_heads, kv_window, mask)


def window_mask(segments, index, rows):
    padding = DEPTH * rows
    base = index * rows
    seg_pad = jnp.concatenate([jnp.full((padding,), -1, jnp.int32), segments])
    seg_query = lax.dynamic_slice_in_dim(segments, base, rows, 0)
    seg_keys = lax.dynamic_slice_in_dim(seg_pad, base, SPAN * rows, 0)
    query_pos = jnp.arange(rows, dtype=jnp.int32)
    key_pos = jnp.arange(SPAN * rows, dtype=jnp.int32) - padding
    allowed = (seg_keys[:, None] == seg_query[None, :]) & (key_pos[:, None] <= query_pos[None, :])
    return jnp.where(allowed, 0.0, MASKED).astype(jnp.bfloat16)


def shift(value, steps):
    count = lax.axis_size("dp")
    first, last = max(0, -steps), min(count, count - steps)
    return lax.ppermute(value, "dp", [(s, s + steps) for s in range(first, last)])


def body(queries, keys, values, grad_out, segments):
    rows = queries.shape[0]
    heads = keys.shape[1] // HEAD_DIM
    index = lax.axis_index("dp")
    mask = window_mask(segments, index, rows)
    kv = jnp.stack([keys.reshape(rows, heads, HEAD_DIM), values.reshape(rows, heads, HEAD_DIM)])
    kv = kv.transpose(2, 0, 1, 3)
    parts = [shift(kv, distance) for distance in range(DEPTH, 0, -1)] + [kv]
    kv_window = jnp.stack(parts)
    grad_heads = lax.all_to_all(grad_out, "head", split_axis=1, concat_axis=0, tiled=True)
    out, grad_queries, dkv = attention(queries, grad_heads, kv_window, mask)
    total = dkv[DEPTH].astype(jnp.float32)
    for distance in range(1, SPAN):
        total = total + shift(dkv[DEPTH - distance], -distance).astype(jnp.float32)
    total = total.astype(jnp.bfloat16).transpose(1, 2, 0, 3).reshape(2, rows, heads * HEAD_DIM)
    attention_out = lax.all_to_all(out, "head", split_axis=0, concat_axis=1, tiled=True)
    return attention_out, grad_queries, total[0], total[1]


def solution(mesh):
    placed = (P("dp", "head"), P("dp", "head"), P("dp", "head"), P(("dp", "head"), None), P())
    return jax.shard_map(
        body,
        mesh=mesh,
        in_specs=placed,
        out_specs=(P(("dp", "head"), None), P("dp", "head"), P("dp", "head"), P("dp", "head")),
        check_vma=False,
    )
```

time: 380 us -> 220 us (0.58)
  the two profiles are of different devices: /device:TPU:0 before, /device:TPU:12 now
where the time goes in v1:
time: 220 us; the launch traced here: 219 us
  waiting for transfers between devices  74.7 us (34%)
  Pallas kernels  59.2 us (27%)
  starting transfers between devices  56.8 us (26%)
  local copies, waits for them, and re-layouts  19.1 us (9%)
  blocking collectives  5 us (2%)
  other arithmetic  3.61 us (2%)
    ppermute x16, waiting for transfers between devices, shift(): lax.ppermute(value, 'dp', [(s, s + steps) for s in range(first, last)])  74.7 us
    pallas_call x1, Pallas kernels, attention(): pl.pallas_call(kernel, grid=(heads,), in_specs=[head_spec, head_spec, kv_...  59.2 us
    ppermute x16, starting transfers between devices, shift(): lax.ppermute(value, 'dp', [(s, s + steps) for s in range(first, last)])  53 us
    unnamed x26, local copies, waits for them, and re-layouts  14.4 us
    all_to_all x1, blocking collectives, body(): lax.all_to_all(out, 'head', split_axis=0, concat_axis=1, tiled=True)  5 us
  transfers between devices with their start and end apart: 17, of which 9 were waited for; matrix products, arithmetic and copies ran while one was open for 7% of the time, Pallas kernels for 0%

profile of v1, /device:TPU:12, one launch (start us, length us, event | category | flops | bytes accessed | tf_op | source)
XLA Modules:
  0.0 219.3 jit_solution(928634527907666382)
XLA Ops:
  3.9 3.4 %collective-permute-start.7 = (bf16[4,2,128,128]{3,2,1,0:T(8,128)(2,1)}, bf16[4,2,128,128]{3,2,1,0:T(8,128)(2,1)}, u32[]{:S(2)}, u32[]{:S(2)}) collective-permute-start(bf16[4,2,128,128]{3,2,1,0:T(8,128)(2,1)} %fusion.10), channel_id=1, source_target_pairs={{0,2},{2,4},{4,6},{6,8},{8,10},{10,12},{12,14},{14,16},{16,18},{18... | collective-permute-start | bytes 786440 | tf_op jit(solution)/shard_map/ppermute | solution.py:185
  7.3 3.4 %collective-permute-start.6 = (bf16[4,2,128,128]{3,2,1,0:T(8,128)(2,1)}, bf16[4,2,128,128]{3,2,1,0:T(8,128)(2,1)}, u32[]{:S(2)}, u32[]{:S(2)}) collective-permute-start(bf16[4,2,128,128]{3,2,1,0:T(8,128)(2,1)} %fusion.10), channel_id=1, source_target_pairs={{0,4},{2,6},{4,8},{6,10},{8,12},{10,14},{12,16},{14,18},{16,20},{1... | collective-permute-start | bytes 786440 | tf_op jit(solution)/shard_map/ppermute | solution.py:185
  10.7 4.4 %collective-permute-start.5 = (bf16[4,2,128,128]{3,2,1,0:T(8,128)(2,1)}, bf16[4,2,128,128]{3,2,1,0:T(8,128)(2,1)}, u32[]{:S(2)}, u32[]{:S(2)}) collective-permute-start(bf16[4,2,128,128]{3,2,1,0:T(8,128)(2,1)} %fusion.10), channel_id=1, source_target_pairs={{0,6},{2,8},{4,10},{6,12},{8,14},{10,16},{12,18},{14,20},{16,22},{... | collective-permute-start | bytes 786440 | tf_op jit(solution)/shard_map/ppermute | solution.py:185
  15.1 2.0 collective-permute-start.1
  17.1 2.0 collective-permute-start
  20.4 3.8 %all-to-all-start = ((bf16[64,2,6144]{2,0,1:T(8,128)(2,1)}), bf16[64,2,6144]{2,0,1:T(8,128)(2,1)S(1)}, u32[]{:S(2)}, u32[]{:S(2)}) async-start(bf16[64,2,6144]{2,0,1:T(8,128)(2,1)} %bitcast.56), calls=%async_computation | async-start | bytes 3145728 | tf_op jit(solution)/shard_map/all_to_all | solution.py:197
  25.2 28.2 %collective-permute-done = bf16[4,2,128,128]{3,2,1,0:T(8,128)(2,1)} collective-permute-done((bf16[4,2,128,128]{3,2,1,0:T(8,128)(2,1)}, bf16[4,2,128,128]{3,2,1,0:T(8,128)(2,1)}, u32[]{:S(2)}, u32[]{:S(2)}) %collective-permute-start) | collective-permute-done | bytes 262176 | tf_op jit(solution)/shard_map/ppermute | solution.py:185
  53.4 1.9 collective-permute-start.2
  55.3 1.7 bitcast_dynamic-update-slice_fusion.8
  57.0 1.9 collective-permute-start.3
  58.9 1.7 bitcast_dynamic-update-slice_fusion.7
  60.5 5.2 %collective-permute-done.2 = bf16[4,2,128,128]{3,2,1,0:T(8,128)(2,1)S(1)} collective-permute-done((bf16[4,2,128,128]{3,2,1,0:T(8,128)(2,1)}, bf16[4,2,128,128]{3,2,1,0:T(8,128)(2,1)S(1)}, u32[]{:S(2)}, u32[]{:S(2)}) %collective-permute-start.2) | collective-permute-done | bytes 262176 | tf_op jit(solution)/shard_map/ppermute | solution.py:185
  65.8 1.9 collective-permute-start.4
  68.4 2.5 %collective-permute-done.3 = bf16[4,2,128,128]{3,2,1,0:T(8,128)(2,1)S(1)} collective-permute-done((bf16[4,2,128,128]{3,2,1,0:T(8,128)(2,1)}, bf16[4,2,128,128]{3,2,1,0:T(8,128)(2,1)S(1)}, u32[]{:S(2)}, u32[]{:S(2)}) %collective-permute-start.3) | collective-permute-done | bytes 262176 | tf_op jit(solution)/shard_map/ppermute | solution.py:185
  71.7 2.6 %collective-permute-done.4 = bf16[4,2,128,128]{3,2,1,0:T(8,128)(2,1)S(1)} collective-permute-done((bf16[4,2,128,128]{3,2,1,0:T(8,128)(2,1)}, bf16[4,2,128,128]{3,2,1,0:T(8,128)(2,1)S(1)}, u32[]{:S(2)}, u32[]{:S(2)}) %collective-permute-start.4) | collective-permute-done | bytes 262176 | tf_op jit(solution)/shard_map/ppermute | solution.py:185
  75.0 1.7 bitcast_dynamic-update-slice_fusion.3
  76.6 1.7 bitcast_dynamic-update-slice_fusion.2
  78.4 1.7 bitcast_dynamic-update-slice_fusion.1
  80.7 59.2 %attention.1 = (bf16[128,6144]{1,0:T(8,128)(2,1)S(1)}, bf16[128,6144]{1,0:T(8,128)(2,1)}, bf16[9,4,2,128,128]{4,3,2,1,0:T(8,128)(2,1)}) custom-call(bf16[128,6144]{1,0:T(8,128)(2,1)S(1)} %copy-done, bf16[128,6144]{1,0:T(8,128)(2,1)S(1)} %bitcast.57, bf16[9,4,2,128,128]{4,3,2,1,0:T(8,128)(2,1)} %bitcast_dynamic-update-slice_fusion.kv_ref, ...), custom_call_target="tpu_custom_call" | custom-call | tf_op jit(solution)/shard_map/attention/pallas_call | solution.py:154
  139.9 1.6 slice_bitcast_fusion.7
  141.6 3.3 %collective-permute-start.8 = (bf16[4,2,128,128]{3,2,1,0:T(8,128)(2,1)S(1)}, bf16[4,2,128,128]{3,2,1,0:T(8,128)(2,1)S(1)}, u32[]{:S(2)}, u32[]{:S(2)}) collective-permute-start(bf16[4,2,128,128]{3,2,1,0:T(8,128)(2,1)S(1)} %get-tuple-element.14), channel_id=1, source_target_pairs={{2,0},{4,2},{6,4},{8,6},{10,8},{12,10},{14,12},{16,14},{18,16},{20... | collective-permute-start | bytes 786440 | tf_op jit(solution)/shard_map/ppermute | solution.py:185
  147.5 1.9 collective-permute-start.13
  149.4 1.9 collective-permute-start.12
  152.2 1.9 collective-permute-start.11
  154.2 2.7 %collective-permute-done.15 = bf16[4,2,128,128]{3,2,1,0:T(8,128)(2,1)S(1)} collective-permute-done((bf16[4,2,128,128]{3,2,1,0:T(8,128)(2,1)S(1)}, bf16[4,2,128,128]{3,2,1,0:T(8,128)(2,1)S(1)}, u32[]{:S(2)}, u32[]{:S(2)}) %collective-permute-start.15) | collective-permute-done | bytes 262176 | tf_op jit(solution)/shard_map/ppermute | solution.py:185
  156.9 8.6 %collective-permute-start.10 = (bf16[4,2,128,128]{3,2,1,0:T(8,128)(2,1)S(1)}, bf16[4,2,128,128]{3,2,1,0:T(8,128)(2,1)S(1)}, u32[]{:S(2)}, u32[]{:S(2)}) collective-permute-start(bf16[4,2,128,128]{3,2,1,0:T(8,128)(2,1)S(1)} %get-tuple-element.20), channel_id=1, source_target_pairs={{6,0},{8,2},{10,4},{12,6},{14,8},{16,10},{18,12},{20,14},{22,16},{... | collective-permute-start | bytes 786440 | tf_op jit(solution)/shard_map/ppermute | solution.py:185
  165.4 11.9 %collective-permute-start.9 = (bf16[4,2,128,128]{3,2,1,0:T(8,128)(2,1)S(1)}, bf16[4,2,128,128]{3,2,1,0:T(8,128)(2,1)S(1)}, u32[]{:S(2)}, u32[]{:S(2)}) collective-permute-start(bf16[4,2,128,128]{3,2,1,0:T(8,128)(2,1)S(1)} %get-tuple-element.21), channel_id=1, source_target_pairs={{4,0},{6,2},{8,4},{10,6},{12,8},{14,10},{16,12},{18,14},{20,16},{2... | collective-permute-start | bytes 786440 | tf_op jit(solution)/shard_map/ppermute | solution.py:185
  177.3 5.0 %all_to_all.38 = bf16[2,64,6144]{2,1,0:T(8,128)(2,1)S(1)} all-to-all(bf16[2,64,6144]{2,1,0:T(8,128)(2,1)S(1)} %bitcast.58), channel_id=1, replica_groups=mesh['dp'=16,'head'=2] {'head'}, dimensions={0} | all-to-all | bytes 3145728 | tf_op jit(solution)/shard_map/all_to_all | solution.py:203
  183.6 4.6 %collective-permute-done.11 = bf16[4,2,128,128]{3,2,1,0:T(8,128)(2,1)S(1)} collective-permute-done((bf16[4,2,128,128]{3,2,1,0:T(8,128)(2,1)S(1)}, bf16[4,2,128,128]{3,2,1,0:T(8,128)(2,1)S(1)}, u32[]{:S(2)}, u32[]{:S(2)}) %collective-permute-start.11) | collective-permute-done | bytes 262176 | tf_op jit(solution)/shard_map/ppermute | solution.py:185
  188.2 11.3 %collective-permute-done.10 = bf16[4,2,128,128]{3,2,1,0:T(8,128)(2,1)S(1)} collective-permute-done((bf16[4,2,128,128]{3,2,1,0:T(8,128)(2,1)S(1)}, bf16[4,2,128,128]{3,2,1,0:T(8,128)(2,1)S(1)}, u32[]{:S(2)}, u32[]{:S(2)}) %collective-permute-start.10) | collective-permute-done | bytes 262176 | tf_op jit(solution)/shard_map/ppermute | solution.py:185
  199.5 16.7 %collective-permute-done.9 = bf16[4,2,128,128]{3,2,1,0:T(8,128)(2,1)S(1)} collective-permute-done((bf16[4,2,128,128]{3,2,1,0:T(8,128)(2,1)S(1)}, bf16[4,2,128,128]{3,2,1,0:T(8,128)(2,1)S(1)}, u32[]{:S(2)}, u32[]{:S(2)}) %collective-permute-start.9) | collective-permute-done | bytes 262176 | tf_op jit(solution)/shard_map/ppermute | solution.py:185
  216.2 1.3 fusion.9
  (44 shorter events, 14.9 us)
Async XLA Ops:
  0.6 18.5 %copy-start.1 = (bf16[64,12288]{1,0:T(8,128)(2,1)S(1)}, bf16[64,12288]{1,0:T(8,128)(2,1)}, u32[]{:S(2)}) copy-start(bf16[64,12288]{1,0:T(8,128)(2,1)} %param.8) | copy-start | bytes 4718596
  1.9 18.5 %copy-start.2 = (bf16[1,128,4,128]{3,1,0,2:T(8,128)(2,1)}, bf16[1,128,4,128]{3,1,0,2:T(8,128)(2,1)S(1)}, u32[]{:S(2)}) copy-start(bf16[1,128,4,128]{3,1,0,2:T(8,128)(2,1)S(1)} %copy.14) | copy-start | bytes 393220
  3.2 17.2 %copy-start.4 = (bf16[1,128,4,128]{3,1,0,2:T(8,128)(2,1)}, bf16[1,128,4,128]{3,1,0,2:T(8,128)(2,1)S(1)}, u32[]{:S(2)}) copy-start(bf16[1,128,4,128]{3,1,0,2:T(8,128)(2,1)S(1)} %copy.15) | copy-start | bytes 393220
  3.9 74.4 %collective-permute-start.7 = (bf16[4,2,128,128]{3,2,1,0:T(8,128)(2,1)}, bf16[4,2,128,128]{3,2,1,0:T(8,128)(2,1)}, u32[]{:S(2)}, u32[]{:S(2)}) collective-permute-start(bf16[4,2,128,128]{3,2,1,0:T(8,128)(2,1)} %fusion.10), channel_id=1, source_target_pairs={{0,2},{2,4},{4,6},{6,8},{8,10},{10,12},{12,14},{14,16},{16,18},{18... | collective-permute-start | bytes 786440 | tf_op jit(solution)/shard_map/ppermute | solution.py:185
  7.3 69.3 %collective-permute-start.6 = (bf16[4,2,128,128]{3,2,1,0:T(8,128)(2,1)}, bf16[4,2,128,128]{3,2,1,0:T(8,128)(2,1)}, u32[]{:S(2)}, u32[]{:S(2)}) collective-permute-start(bf16[4,2,128,128]{3,2,1,0:T(8,128)(2,1)} %fusion.10), channel_id=1, source_target_pairs={{0,4},{2,6},{4,8},{6,10},{8,12},{10,14},{12,16},{14,18},{16,20},{1... | collective-permute-start | bytes 786440 | tf_op jit(solution)/shard_map/ppermute | solution.py:185
  10.7 64.2 %collective-permute-start.5 = (bf16[4,2,128,128]{3,2,1,0:T(8,128)(2,1)}, bf16[4,2,128,128]{3,2,1,0:T(8,128)(2,1)}, u32[]{:S(2)}, u32[]{:S(2)}) collective-permute-start(bf16[4,2,128,128]{3,2,1,0:T(8,128)(2,1)} %fusion.10), channel_id=1, source_target_pairs={{0,6},{2,8},{4,10},{6,12},{8,14},{10,16},{12,18},{14,20},{16,22},{... | collective-permute-start | bytes 786440 | tf_op jit(solution)/shard_map/ppermute | solution.py:185
  15.1 41.9 %collective-permute-start.1 = (bf16[4,2,128,128]{3,2,1,0:T(8,128)(2,1)}, bf16[4,2,128,128]{3,2,1,0:T(8,128)(2,1)}, u32[]{:S(2)}, u32[]{:S(2)}) collective-permute-start(bf16[4,2,128,128]{3,2,1,0:T(8,128)(2,1)} %fusion.10), channel_id=1, source_target_pairs={{0,14},{2,16},{4,18},{6,20},{8,22},{10,24},{12,26},{14,28},{16,30}... | collective-permute-start | bytes 786440 | tf_op jit(solution)/shard_map/ppermute | solution.py:185
  17.1 36.2 %collective-permute-start = (bf16[4,2,128,128]{3,2,1,0:T(8,128)(2,1)}, bf16[4,2,128,128]{3,2,1,0:T(8,128)(2,1)}, u32[]{:S(2)}, u32[]{:S(2)}) collective-permute-start(bf16[4,2,128,128]{3,2,1,0:T(8,128)(2,1)} %fusion.10), channel_id=1, source_target_pairs={{0,16},{2,18},{4,20},{6,22},{8,24},{10,26},{12,28},{14,30},{1,17},... | collective-permute-start | bytes 786440 | tf_op jit(solution)/shard_map/ppermute | solution.py:185
  20.4 3.8 %copy-start.6 = (s32[2048]{0:T(1024)S(1)}, s32[2048]{0:T(1024)}, u32[]{:S(2)}) copy-start(s32[2048]{0:T(1024)} %param.9) | copy-start | bytes 24580
  20.4 60.4 %all-to-all-start = ((bf16[64,2,6144]{2,0,1:T(8,128)(2,1)}), bf16[64,2,6144]{2,0,1:T(8,128)(2,1)S(1)}, u32[]{:S(2)}, u32[]{:S(2)}) async-start(bf16[64,2,6144]{2,0,1:T(8,128)(2,1)} %bitcast.56), calls=%async_computation | async-start | bytes 3145728 | tf_op jit(solution)/shard_map/all_to_all | solution.py:197
  24.2 55.8 %copy-start.3 = (bf16[1,128,4,128]{3,1,0,2:T(8,128)(2,1)S(1)}, bf16[1,128,4,128]{3,1,0,2:T(8,128)(2,1)}, u32[]{:S(2)}) copy-start(bf16[1,128,4,128]{3,1,0,2:T(8,128)(2,1)} %copy-done.2) | copy-start | bytes 393220
  24.2 55.8 %copy-start.5 = (bf16[1,128,4,128]{3,1,0,2:T(8,128)(2,1)S(1)}, bf16[1,128,4,128]{3,1,0,2:T(8,128)(2,1)}, u32[]{:S(2)}) copy-start(bf16[1,128,4,128]{3,1,0,2:T(8,128)(2,1)} %copy-done.4) | copy-start | bytes 393220
  25.2 55.6 %copy-start = (bf16[128,6144]{1,0:T(8,128)(2,1)S(1)}, bf16[128,6144]{1,0:T(8,128)(2,1)}, u32[]{:S(2)}) copy-start(bf16[128,6144]{1,0:T(8,128)(2,1)} %q_ref.1) | copy-start | bytes 4718596
  53.4 12.4 %collective-permute-start.2 = (bf16[4,2,128,128]{3,2,1,0:T(8,128)(2,1)}, bf16[4,2,128,128]{3,2,1,0:T(8,128)(2,1)S(1)}, u32[]{:S(2)}, u32[]{:S(2)}) collective-permute-start(bf16[4,2,128,128]{3,2,1,0:T(8,128)(2,1)} %fusion.10), channel_id=1, source_target_pairs={{0,12},{2,14},{4,16},{6,18},{8,20},{10,22},{12,24},{14,26},{16,28}... | collective-permute-start | bytes 786440 | tf_op jit(solution)/shard_map/ppermute | solution.py:185
  57.0 14.0 %collective-permute-start.3 = (bf16[4,2,128,128]{3,2,1,0:T(8,128)(2,1)}, bf16[4,2,128,128]{3,2,1,0:T(8,128)(2,1)S(1)}, u32[]{:S(2)}, u32[]{:S(2)}) collective-permute-start(bf16[4,2,128,128]{3,2,1,0:T(8,128)(2,1)} %fusion.10), channel_id=1, source_target_pairs={{0,10},{2,12},{4,14},{6,16},{8,18},{10,20},{12,22},{14,24},{16,26}... | collective-permute-start | bytes 786440 | tf_op jit(solution)/shard_map/ppermute | solution.py:185
  65.8 8.5 %collective-permute-start.4 = (bf16[4,2,128,128]{3,2,1,0:T(8,128)(2,1)}, bf16[4,2,128,128]{3,2,1,0:T(8,128)(2,1)S(1)}, u32[]{:S(2)}, u32[]{:S(2)}) collective-permute-start(bf16[4,2,128,128]{3,2,1,0:T(8,128)(2,1)} %fusion.10), channel_id=1, source_target_pairs={{0,8},{2,10},{4,12},{6,14},{8,16},{10,18},{12,20},{14,22},{16,24},... | collective-permute-start | bytes 786440 | tf_op jit(solution)/shard_map/ppermute | solution.py:185
  141.6 10.7 %collective-permute-start.8 = (bf16[4,2,128,128]{3,2,1,0:T(8,128)(2,1)S(1)}, bf16[4,2,128,128]{3,2,1,0:T(8,128)(2,1)S(1)}, u32[]{:S(2)}, u32[]{:S(2)}) collective-permute-start(bf16[4,2,128,128]{3,2,1,0:T(8,128)(2,1)S(1)} %get-tuple-element.14), channel_id=1, source_target_pairs={{2,0},{4,2},{6,4},{8,6},{10,8},{12,10},{14,12},{16,14},{18,16},{20... | collective-permute-start | bytes 786440 | tf_op jit(solution)/shard_map/ppermute | solution.py:185
  144.9 12.0 %collective-permute-start.15 = (bf16[4,2,128,128]{3,2,1,0:T(8,128)(2,1)S(1)}, bf16[4,2,128,128]{3,2,1,0:T(8,128)(2,1)S(1)}, u32[]{:S(2)}, u32[]{:S(2)}) collective-permute-start(bf16[4,2,128,128]{3,2,1,0:T(8,128)(2,1)S(1)} %get-tuple-element.15), channel_id=1, source_target_pairs={{16,0},{18,2},{20,4},{22,6},{24,8},{26,10},{28,12},{30,14},{17,1},... | collective-permute-start | bytes 786440 | tf_op jit(solution)/shard_map/ppermute | solution.py:185
  146.2 19.2 %collective-permute-start.14 = (bf16[4,2,128,128]{3,2,1,0:T(8,128)(2,1)S(1)}, bf16[4,2,128,128]{3,2,1,0:T(8,128)(2,1)S(1)}, u32[]{:S(2)}, u32[]{:S(2)}) collective-permute-start(bf16[4,2,128,128]{3,2,1,0:T(8,128)(2,1)S(1)} %get-tuple-element.16), channel_id=1, source_target_pairs={{14,0},{16,2},{18,4},{20,6},{22,8},{24,10},{26,12},{28,14},{30,16}... | collective-permute-start | bytes 786440 | tf_op jit(solution)/shard_map/ppermute | solution.py:185
  147.5 36.1 %collective-permute-start.13 = (bf16[4,2,128,128]{3,2,1,0:T(8,128)(2,1)S(1)}, bf16[4,2,128,128]{3,2,1,0:T(8,128)(2,1)S(1)}, u32[]{:S(2)}, u32[]{:S(2)}) collective-permute-start(bf16[4,2,128,128]{3,2,1,0:T(8,128)(2,1)S(1)} %get-tuple-element.17), channel_id=1, source_target_pairs={{12,0},{14,2},{16,4},{18,6},{20,8},{22,10},{24,12},{26,14},{28,16}... | collective-permute-start | bytes 786440 | tf_op jit(solution)/shard_map/ppermute | solution.py:185
  149.4 34.1 %collective-permute-start.12 = (bf16[4,2,128,128]{3,2,1,0:T(8,128)(2,1)S(1)}, bf16[4,2,128,128]{3,2,1,0:T(8,128)(2,1)S(1)}, u32[]{:S(2)}, u32[]{:S(2)}) collective-permute-start(bf16[4,2,128,128]{3,2,1,0:T(8,128)(2,1)S(1)} %get-tuple-element.18), channel_id=1, source_target_pairs={{10,0},{12,2},{14,4},{16,6},{18,8},{20,10},{22,12},{24,14},{26,16}... | collective-permute-start | bytes 786440 | tf_op jit(solution)/shard_map/ppermute | solution.py:185
  152.2 36.0 %collective-permute-start.11 = (bf16[4,2,128,128]{3,2,1,0:T(8,128)(2,1)S(1)}, bf16[4,2,128,128]{3,2,1,0:T(8,128)(2,1)S(1)}, u32[]{:S(2)}, u32[]{:S(2)}) collective-permute-start(bf16[4,2,128,128]{3,2,1,0:T(8,128)(2,1)S(1)} %get-tuple-element.19), channel_id=1, source_target_pairs={{8,0},{10,2},{12,4},{14,6},{16,8},{18,10},{20,12},{22,14},{24,16},... | collective-permute-start | bytes 786440 | tf_op jit(solution)/shard_map/ppermute | solution.py:185
  156.9 42.6 %collective-permute-start.10 = (bf16[4,2,128,128]{3,2,1,0:T(8,128)(2,1)S(1)}, bf16[4,2,128,128]{3,2,1,0:T(8,128)(2,1)S(1)}, u32[]{:S(2)}, u32[]{:S(2)}) collective-permute-start(bf16[4,2,128,128]{3,2,1,0:T(8,128)(2,1)S(1)} %get-tuple-element.20), channel_id=1, source_target_pairs={{6,0},{8,2},{10,4},{12,6},{14,8},{16,10},{18,12},{20,14},{22,16},{... | collective-permute-start | bytes 786440 | tf_op jit(solution)/shard_map/ppermute | solution.py:185
  165.4 50.7 %collective-permute-start.9 = (bf16[4,2,128,128]{3,2,1,0:T(8,128)(2,1)S(1)}, bf16[4,2,128,128]{3,2,1,0:T(8,128)(2,1)S(1)}, u32[]{:S(2)}, u32[]{:S(2)}) collective-permute-start(bf16[4,2,128,128]{3,2,1,0:T(8,128)(2,1)S(1)} %get-tuple-element.21), channel_id=1, source_target_pairs={{4,0},{6,2},{8,4},{10,6},{12,8},{14,10},{16,12},{18,14},{20,16},{2... | collective-permute-start | bytes 786440 | tf_op jit(solution)/shard_map/ppermute | solution.py:185

commit v2 on v1

--- a/solution.py
+++ b/solution.py
@@ -119,52 +119,168 @@
     ]
 
 
-def kernel(q_ref, g_ref, kv_ref, mask_ref, out_ref, dq_ref, dkv_ref, *tmp):
-    @pl.when(pl.program_id(0) == 0)
-    def _():
-        fill_constants(mask_ref, tmp)
-
-    def at(ref, h):
-        return ref[:, h * HEAD_DIM : (h + 1) * HEAD_DIM]
-
-    def put(ref, h, value):
-        ref[:, pl.ds(pl.multiple_of(h * HEAD_DIM, HEAD_DIM), HEAD_DIM)] = value
-
-    def put_block(which, j, value):
-        dkv_ref[j, 0, which] = value
-
-    attend_group(
-        functools.partial(at, q_ref),
-        functools.partial(at, g_ref),
-        lambda j: kv_ref[j, 0, 0],
-        lambda j: kv_ref[j, 0, 1],
-        functools.partial(put, out_ref),
-        functools.partial(put, dq_ref),
-        functools.partial(put_block, 0),
-        functools.partial(put_block, 1),
-        tmp,
-    )
-
-
-def attention(queries, grad_heads, kv_window, mask):
+MESH = pl.DeviceIdType.MESH
+
+
+def kernel(count, q_ref, grad_ref, key_ref, value_ref, mask_ref, out_ref, dq_ref, dk_ref, dv_ref,
+           window, partial, arrived, g_heads, o_heads, o_arrived,
+           kv_send, kv_recv, part_send, part_recv, g_send, g_recv, o_send, o_recv, *tmp):
+    me, core = lax.axis_index("dp"), lax.axis_index("head")
+    heads = window.shape[0]
+    half, columns = grad_ref.shape[0], q_ref.shape[1]
+    width = GROUP * HEAD_DIM
+
+    def lanes(start, size):
+        return pl.ds(pl.multiple_of(start, HEAD_DIM), size)
+
+    mine, other = core * columns, (1 - core) * columns
+    my_rows = pl.ds(pl.multiple_of(core * half, half), half)
+    other_rows = pl.ds(pl.multiple_of((1 - core) * half, half), half)
+
+    def kv_copy(h, d):
+        return pltpu.make_async_remote_copy(
+            window.at[h, DEPTH], window.at[h, DEPTH - d], kv_send.at[h, d - 1], kv_recv.at[h, d - 1],
+            device_id=(lax.rem(me + d, count), core), device_id_type=MESH)
+
+    def part_copy(h, d):
+        return pltpu.make_async_remote_copy(
+            partial.at[h, DEPTH - d], arrived.at[h, d - 1], part_send.at[h, d - 1], part_recv.at[h, d - 1],
+            device_id=(lax.rem(me - d + count, count), core), device_id_type=MESH)
+
+    def g_copy(h):
+        return pltpu.make_async_remote_copy(
+            grad_ref.at[:, lanes(other + h * width, width)], g_heads.at[my_rows, lanes(h * width, width)],
+            g_send.at[h], g_recv.at[h], device_id=(me, 1 - core), device_id_type=MESH)
+
+    def o_copy(h):
+        return pltpu.make_async_remote_copy(
+            o_heads.at[other_rows, lanes(h * width, width)], o_arrived.at[:, lanes(h * width, width)],
+            o_send.at[h], o_recv.at[h], device_id=(me, 1 - core), device_id_type=MESH)
+
+    barrier = pltpu.get_barrier_semaphore()
+    pl.semaphore_signal(barrier, inc=1, device_id=(me, 1 - core), device_id_type=MESH)
+    for d in range(1, SPAN):
+        @pl.when(me + d < count)
+        def _():
+            pl.semaphore_signal(barrier, inc=1, device_id=(lax.rem(me + d, count), core), device_id_type=MESH)
+
+        @pl.when(me >= d)
+        def _():
+            pl.semaphore_signal(barrier, inc=1, device_id=(lax.rem(me - d + count, count), core), device_id_type=MESH)
+
+    for h in range(heads):
+        window[h, DEPTH, 0] = key_ref[:, h * HEAD_DIM : (h + 1) * HEAD_DIM]
+        window[h, DEPTH, 1] = value_ref[:, h * HEAD_DIM : (h + 1) * HEAD_DIM]
+    for d in range(1, SPAN):
+        @pl.when(me < d)
+        def _():
+            window[:, DEPTH - d] = jnp.zeros((heads,) + window.shape[2:], jnp.bfloat16)
+
+    pl.semaphore_wait(barrier, 1 + jnp.minimum(me, DEPTH) + jnp.minimum(count - 1 - me, DEPTH))
+
+    def start_head(h, carry):
+        g_copy(h).start()
+        for d in range(1, SPAN):
+            @pl.when(me + d < count)
+            def _():
+                kv_copy(h, d).start()
+        return carry
+
+    lax.fori_loop(0, heads, start_head, 0)
+    g_heads[my_rows, :] = grad_ref[:, lanes(mine, columns)]
+    fill_constants(mask_ref, tmp)
+
+    def head_step(h, carry):
+        g_copy(h).wait_recv()
+        for d in range(1, SPAN):
+            @pl.when(me >= d)
+            def _():
+                kv_copy(h, d).wait_recv()
+
+        def at(ref, g):
+            return ref[:, lanes(h * width + g * HEAD_DIM, HEAD_DIM)]
+
+        def put(ref, g, value):
+            ref[:, lanes(h * width + g * HEAD_DIM, HEAD_DIM)] = value
+
+        def put_block(which, j, value):
+            partial[h, j, which] = value
+
+        attend_group(
+            functools.partial(at, q_ref),
+            functools.partial(at, g_heads),
+            lambda j: window[h, j, 0],
+            lambda j: window[h, j, 1],
+            functools.partial(put, o_heads),
+            functools.partial(put, dq_ref),
+            functools.partial(put_block, 0),
+            functools.partial(put_block, 1),
+            tmp,
+        )
+        for d in range(1, SPAN):
+            @pl.when(me >= d)
+            def _():
+                part_copy(h, d).start()
+        o_copy(h).start()
+        out_ref[:, lanes(mine + h * width, width)] = o_heads[my_rows, lanes(h * width, width)]
+        return carry
+
+    lax.fori_loop(0, heads, head_step, 0)
+
+    def finish_head(h, carry):
+        g_copy(h).wait_send()
+        o_copy(h).wait()
+        for d in range(1, SPAN):
+            @pl.when(me + d < count)
+            def _():
+                kv_copy(h, d).wait_send()
+                part_copy(h, d).wait_recv()
+
+            @pl.when(me + d >= count)
+            def _():
+                arrived[h, d - 1] = jnp.zeros(arrived.shape[2:], jnp.bfloat16)
+
+            @pl.when(me >= d)
+            def _():
+                part_copy(h, d).wait_send()
+
+        total = partial[h, DEPTH].astype(jnp.float32)
+        for d in range(1, SPAN):
+            total = total + arrived[h, d - 1].astype(jnp.float32)
+        dk_ref[:, lanes(h * HEAD_DIM, HEAD_DIM)] = total[0].astype(jnp.bfloat16)
+        dv_ref[:, lanes(h * HEAD_DIM, HEAD_DIM)] = total[1].astype(jnp.bfloat16)
+        return carry
+
+    lax.fori_loop(0, heads, finish_head, 0)
+    out_ref[:, lanes(other, columns)] = o_arrived[...]
+
+
+def attention(count, queries, grad_out, keys, values, mask):
     rows, columns = queries.shape
-    heads = columns // (GROUP * HEAD_DIM)
-    head_spec = pl.BlockSpec((rows, GROUP * HEAD_DIM), lambda h: (0, h))
-    kv_spec = pl.BlockSpec((SPAN, 1, 2, rows, HEAD_DIM), lambda h: (0, h, 0, 0, 0))
+    heads = keys.shape[1] // HEAD_DIM
+    half = grad_out.shape[0]
+    tile = (2, rows, HEAD_DIM)
+    sems = pltpu.SemaphoreType.DMA
+    in_vmem = pl.BlockSpec(memory_space=pltpu.VMEM)
     return pl.pallas_call(
-        kernel,
-        grid=(heads,),
-        in_specs=[head_spec, head_spec, kv_spec, pl.BlockSpec(mask.shape, lambda h: (0, 0))],
-        out_specs=[head_spec, head_spec, kv_spec],
-        out_shape=[
-            jax.ShapeDtypeStruct(queries.shape, jnp.bfloat16),
-            jax.ShapeDtypeStruct(queries.shape, jnp.bfloat16),
-            jax.ShapeDtypeStruct(kv_window.shape, jnp.bfloat16),
-        ],
-        scratch_shapes=scratch(rows),
-        compiler_params=pltpu.CompilerParams(vmem_limit_bytes=48 * 1024 * 1024),
+        functools.partial(kernel, count),
+        in_specs=[in_vmem] * 5,
+        out_specs=[in_vmem] * 4,
+        out_shape=[jax.ShapeDtypeStruct(a.shape, jnp.bfloat16) for a in (grad_out, queries, keys, values)],
+        scratch_shapes=[
+            pltpu.VMEM((heads, SPAN) + tile, jnp.bfloat16),
+            pltpu.VMEM((heads, SPAN) + tile, jnp.bfloat16),
+            pltpu.VMEM((heads, DEPTH) + tile, jnp.bfloat16),
+            pltpu.VMEM((rows, columns), jnp.bfloat16),
+            pltpu.VMEM((rows, columns), jnp.bfloat16),
+            pltpu.VMEM((half, columns), jnp.bfloat16),
+            sems((heads, DEPTH)), sems((heads, DEPTH)), sems((heads, DEPTH)), sems((heads, DEPTH)),
+            sems((heads,)), sems((heads,)), sems((heads,)), sems((heads,)),
+        ] + scratch(rows),
+        compiler_params=pltpu.CompilerParams(
+            vmem_limit_bytes=56 * 1024 * 1024, collective_id=0, has_side_effects=True),
         name="attention",
-    )(queries, grad_heads, kv_window, mask)
+    )(queries, grad_out, keys, values, mask)
 
 
 def window_mask(segments, index, rows):
@@ -179,29 +295,9 @@
     return jnp.where(allowed, 0.0, MASKED).astype(jnp.bfloat16)
 
 
-def shift(value, steps):
-    count = lax.axis_size("dp")
-    first, last = max(0, -steps), min(count, count - steps)
-    return lax.ppermute(value, "dp", [(s, s + steps) for s in range(first, last)])
-
-
 def body(queries, keys, values, grad_out, segments):
-    rows = queries.shape[0]
-    heads = keys.shape[1] // HEAD_DIM
-    index = lax.axis_index("dp")
-    mask = window_mask(segments, index, rows)
-    kv = jnp.stack([keys.reshape(rows, heads, HEAD_DIM), values.reshape(rows, heads, HEAD_DIM)])
-    kv = kv.transpose(2, 0, 1, 3)
-    parts = [shift(kv, distance) for distance in range(DEPTH, 0, -1)] + [kv]
-    kv_window = jnp.stack(parts)
-    grad_heads = lax.all_to_all(grad_out, "head", split_axis=1, concat_axis=0, tiled=True)
-    out, grad_queries, dkv = attention(queries, grad_heads, kv_window, mask)
-    total = dkv[DEPTH].astype(jnp.float32)
-    for distance in range(1, SPAN):
-        total = total + shift(dkv[DEPTH - distance], -distance).astype(jnp.float32)
-    total = total.astype(jnp.bfloat16).transpose(1, 2, 0, 3).reshape(2, rows, heads * HEAD_DIM)
-    attention_out = lax.all_to_all(out, "head", split_axis=0, concat_axis=1, tiled=True)
-    return attention_out, grad_queries, total[0], total[1]
+    mask = window_mask(segments, lax.axis_index("dp"), queries.shape[0])
+    return tuple(attention(lax.axis_size("dp"), queries, grad_out, keys, values, mask))
 
 
 def solution(mesh):

time: 220 us -> 118 us (0.54)
  the two profiles are of different devices: /device:TPU:12 before, /device:TPU:0 now
where the time goes in v2:
time: 118 us; the launch traced here: 117 us
  Pallas kernels  109 us (92%)
  local copies, waits for them, and re-layouts  6 us (5%)
  other arithmetic  2.17 us (2%)
    pallas_call x1, Pallas kernels, attention(): pl.pallas_call(functools.partial(kernel, count), in_specs=[in_vmem] * 5,...  109 us
    unnamed x10, local copies, waits for them, and re-layouts  5.23 us

profile of v2, /device:TPU:0, one launch (start us, length us, event | category | flops | bytes accessed | tf_op | source)
XLA Modules:
  0.0 117.4 jit_solution(14697823031637617548)
XLA Ops:
  0.6 0.8 dynamic_slice.7
  1.4 0.8 pad_dynamic-slice_fusion
  2.2 1.4 %select_convert_fusion.mask_ref = bf16[1152,128]{1,0:T(8,128)(2,1)} fusion(s32[1152]{0:T(1024)S(1)} %get-tuple-element.5, s32[128]{0:T(128)S(1)} %dynamic_slice.7, s32[1152]{0:T(1024)S(1)} %get-tuple-element.4), kind=kLoop, calls=%fused_computation | loop fusion | flops 737280 | bytes 304640 | tf_op jit(solution)/shard_map/convert_element_type | solution.py:295
  3.6 108.6 %attention.1 = (bf16[64,12288]{1,0:T(8,128)(2,1)}, bf16[128,6144]{1,0:T(8,128)(2,1)}, bf16[128,512]{1,0:T(8,128)(2,1)}, bf16[128,512]{1,0:T(8,128)(2,1)}) custom-call(bf16[128,6144]{1,0:T(8,128)(2,1)} %q_ref.1, bf16[64,12288]{1,0:T(8,128)(2,1)} %grad_ref.1, bf16[128,512]{1,0:T(8,128)(2,1)} %key_ref.1, bf16[128,512]{1,0:T(8,128)(2,1)} %value_ref.1, ...), custom_call_target="tpu_custom_call" | custom-call | tf_op jit(solution)/shard_map/attention/pallas_call | solution.py:265
  112.2 0.0 copy-start
  112.2 2.8 %copy.13 = bf16[64,12288]{1,0:T(8,128)(2,1)} copy(bf16[64,12288]{1,0:T(8,128)(2,1)} %get-tuple-element.10) | data formatting | bytes 3145728
  115.0 0.0 copy-done
  115.0 0.0 copy-start.2
  115.0 0.0 copy-start.1
  115.0 1.1 copy.14
  116.1 0.0 copy-done.2
  116.1 0.7 copy.15
  116.8 0.0 copy-done.1
  116.8 0.7 copy.16
Async XLA Ops:
  112.2 2.8 %copy-start = (bf16[128,6144]{1,0:T(8,128)(2,1)S(1)}, bf16[128,6144]{1,0:T(8,128)(2,1)}, u32[]{:S(2)}) copy-start(bf16[128,6144]{1,0:T(8,128)(2,1)} %get-tuple-element.11) | copy-start | bytes 4718596
  115.0 1.1 copy-start.2
  115.0 1.8 %copy-start.1 = (bf16[128,512]{1,0:T(8,128)(2,1)S(1)}, bf16[128,512]{1,0:T(8,128)(2,1)}, u32[]{:S(2)}) copy-start(bf16[128,512]{1,0:T(8,128)(2,1)} %get-tuple-element.13) | copy-start | bytes 393220

commit v3 on v2

v3 whole, which is shorter than its diff:
```python
import functools
import math

import jax
import jax.numpy as jnp
from jax import lax
from jax.experimental import pallas as pl
from jax.experimental.pallas import tpu as pltpu
from jax.sharding import PartitionSpec as P

QHEADS = 96
KVHEADS = 8
HEAD_DIM = 128
DEPTH = 8
SPAN = DEPTH + 1
RING = DEPTH // 2
GROUP = QHEADS // KVHEADS
MASKED = -(2.0**100)
SCALE = 1.0 / math.sqrt(HEAD_DIM)
NT = (((1,), (1,)), ((), ()))


def dot(a, b):
    return jnp.dot(a, b, preferred_element_type=jnp.float32)


def dot_nt(a, b):
    return lax.dot_general(a, b, NT, preferred_element_type=jnp.float32)


def attend_group(q_at, g_at, k_at, v_at, put_out, put_dq, put_dk, put_dv, tmp):
    (k_aug, v_aug, k_t, v_t, q_aug, g_aug, q_norm, g_norm, p_all, ds_all) = tmp[:10]
    scores, slopes = tmp[10:12], tmp[12:14]
    rows = HEAD_DIM
    for j in range(SPAN):
        at = pl.ds(j * rows, rows)
        k_j, v_j = k_at(j), v_at(j)
        k_aug[at, :HEAD_DIM] = k_j
        v_aug[at, :HEAD_DIM] = v_j
        k_t[:, j * rows : (j + 1) * rows] = k_j.T
        v_t[:HEAD_DIM, j * rows : (j + 1) * rows] = v_j.T
    for h in range(GROUP):
        spot = (h // 4, pl.ds(h % 4 * rows, rows), slice(0, HEAD_DIM))
        q_aug[spot] = q_at(h)
        g_aug[spot] = g_at(h)

    two = 2 * rows
    lane = lax.broadcasted_iota(jnp.int32, (two, HEAD_DIM), 1)

    def quad_step(i, carry):
        at = [slice(t * two, (t + 1) * two) for t in range(2)]
        inv_t = [None, None]

        def softmax(t):
            score = scores[t]
            top = score[0:rows, :].reshape(rows // 8, 8, two).max(axis=0)
            for j in range(1, SPAN):
                part = score[j * rows : (j + 1) * rows, :]
                top = jnp.maximum(top, part.reshape(rows // 8, 8, two).max(axis=0))
            top = jnp.max(top, axis=0, keepdims=True)
            for j in range(SPAN):
                part = score[j * rows : (j + 1) * rows, :]
                e = jnp.exp2((part - top) * (SCALE * math.log2(math.e)))
                p_all[i, j * rows : (j + 1) * rows, at[t]] = e.astype(jnp.bfloat16)

        def output(t):
            both = dot(v_t[...], p_all[i, :, at[t]])
            inv = 1.0 / both[HEAD_DIM : HEAD_DIM + 1]
            inv_t[t] = jnp.broadcast_to(inv, (HEAD_DIM, two)).T
            out = (both[:HEAD_DIM].T * inv_t[t]).astype(jnp.bfloat16)
            put_out(4 * i + 2 * t, out[:rows])
            put_out(4 * i + 2 * t + 1, out[rows:])
            g_pair = g_aug[i, at[t], :HEAD_DIM].astype(jnp.float32)
            delta = -jnp.sum(g_pair * out.astype(jnp.float32), axis=1, keepdims=True)
            hi = delta.astype(jnp.bfloat16).astype(jnp.float32)
            mid = (delta - hi).astype(jnp.bfloat16).astype(jnp.float32)
            low = delta - hi - mid
            tail = jnp.where(lane == 0, hi, jnp.where(lane == 1, mid, jnp.where(lane == 2, low, 0.0)))
            g_aug[i, at[t], HEAD_DIM:] = tail.astype(jnp.bfloat16)
            q_pair = q_aug[i, at[t], :HEAD_DIM].astype(jnp.float32)
            q_norm[i, at[t], :] = (q_pair * inv_t[t]).astype(jnp.bfloat16)
            g_norm[i, at[t], :] = (g_pair * inv_t[t]).astype(jnp.bfloat16)

        def grad_weights(t):
            slopes[t][...] = dot_nt(v_aug[...], g_aug[i, at[t], :])

        def grad_scores(t):
            for j in range(SPAN):
                keys = slice(j * rows, (j + 1) * rows)
                slope = slopes[t][keys, :].astype(jnp.bfloat16)
                ds_all[i, keys, at[t]] = p_all[i, keys, at[t]] * slope

        def grad_query(t):
            dq = (dot(k_t[...], ds_all[i, :, at[t]]).T * (inv_t[t] * SCALE)).astype(jnp.bfloat16)
            put_dq(4 * i + 2 * t, dq[:rows])
            put_dq(4 * i + 2 * t + 1, dq[rows:])

        scores[0][...] = dot_nt(k_aug[...], q_aug[i, at[0], :])
        softmax(0)
        scores[1][...] = dot_nt(k_aug[...], q_aug[i, at[1], :])
        output(0)
        softmax(1)
        grad_weights(0)
        output(1)
        grad_scores(0)
        grad_weights(1)
        grad_query(0)
        grad_scores(1)
        grad_query(1)
        return carry

    lax.fori_loop(0, GROUP // 4, quad_step, 0)
    for j in range(0, SPAN, 3):
        keys = slice(j * rows, (j + 3) * rows)
        dk = sum(dot(ds_all[i, keys, :], q_norm[i]) for i in range(GROUP // 4))
        dv = sum(dot(p_all[i, keys, :], g_norm[i]) for i in range(GROUP // 4))
        for b in range(3):
            put_dk(j + b, (SCALE * dk[b * rows : (b + 1) * rows]).astype(jnp.bfloat16))
            put_dv(j + b, dv[b * rows : (b + 1) * rows].astype(jnp.bfloat16))


def block_mask(seg_ref, me, j):
    rows = seg_ref.shape[1]
    key_block = me - DEPTH + j
    square = (rows, rows)
    key_seg = jnp.broadcast_to(seg_ref[pl.ds(jnp.maximum(key_block, 0), 1), :], square).T
    query_seg = jnp.broadcast_to(seg_ref[pl.ds(me, 1), :], square)
    behind = lax.broadcasted_iota(jnp.int32, square, 0) - lax.broadcasted_iota(jnp.int32, square, 1)
    allowed = (key_seg == query_seg) & (behind <= rows * (DEPTH - j))
    return jnp.where(allowed & (key_block >= 0), 0.0, MASKED).astype(jnp.bfloat16)


def fill_constants(seg_ref, me, tmp):
    k_aug, v_aug, v_t, q_aug = tmp[0], tmp[1], tmp[3], tmp[4]
    v_t[HEAD_DIM:, :] = jnp.ones((v_t.shape[0] - HEAD_DIM, v_t.shape[1]), jnp.bfloat16)
    for j in range(SPAN):
        k_aug[j * HEAD_DIM : (j + 1) * HEAD_DIM, HEAD_DIM:] = block_mask(seg_ref, me, j)
    ones = lax.broadcasted_iota(jnp.int32, (v_aug.shape[0], HEAD_DIM), 1) < 3
    v_aug[:, HEAD_DIM:] = jnp.where(ones, 1.0, 0.0).astype(jnp.bfloat16)
    side = (HEAD_DIM, HEAD_DIM)
    eye = lax.broadcasted_iota(jnp.int32, side, 0) == lax.broadcasted_iota(jnp.int32, side, 1)
    for h in range(GROUP):
        spot = (h // 4, pl.ds(h % 4 * HEAD_DIM, HEAD_DIM), slice(HEAD_DIM, None))
        q_aug[spot] = jnp.where(eye, 1.0, 0.0).astype(jnp.bfloat16)


def scratch(rows):
    window, quads, four = SPAN * rows, GROUP // 4, 4 * rows
    return [
        pltpu.VMEM((window, 2 * HEAD_DIM), jnp.bfloat16),
        pltpu.VMEM((window, 2 * HEAD_DIM), jnp.bfloat16),
        pltpu.VMEM((HEAD_DIM, window), jnp.bfloat16),
        pltpu.VMEM((HEAD_DIM + 16, window), jnp.bfloat16),
        pltpu.VMEM((quads, four, 2 * HEAD_DIM), jnp.bfloat16),
        pltpu.VMEM((quads, four, 2 * HEAD_DIM), jnp.bfloat16),
        pltpu.VMEM((quads, four, HEAD_DIM), jnp.bfloat16),
        pltpu.VMEM((quads, four, HEAD_DIM), jnp.bfloat16),
        pltpu.VMEM((quads, window, four), jnp.bfloat16),
        pltpu.VMEM((quads, window, four), jnp.bfloat16),
    ] + [pltpu.VMEM((window, 2 * rows), jnp.float32)] * 4


MESH = pl.DeviceIdType.MESH


def kernel(count, q_ref, grad_ref, key_ref, value_ref, seg_ref, out_ref, dq_ref, dk_ref, dv_ref,
           window, partial, first_in, second_in, far_out, far_in, near_out, near_in, total,
           g_heads, o_heads, o_arrived,
           kv_send, kv_recv, first_send, first_recv, second_send, second_recv,
           far_send, far_recv, near_send, near_recv, g_send, g_recv, o_send, o_recv, *tmp):
    me, core = lax.axis_index("dp"), lax.axis_index("head")
    spot = lax.rem(me, RING)
    heads = window.shape[0]
    half, columns = grad_ref.shape[0], q_ref.shape[1]
    width = GROUP * HEAD_DIM
    below, above = me >= RING, me + RING < count
    two_below = me >= 2 * RING

    def lanes(start, size):
        return pl.ds(pl.multiple_of(start, HEAD_DIM), size)

    mine, other = core * columns, (1 - core) * columns
    my_rows = pl.ds(pl.multiple_of(core * half, half), half)
    other_rows = pl.ds(pl.multiple_of((1 - core) * half, half), half)

    def remote(source, target, send, recv, place, side=None):
        return pltpu.make_async_remote_copy(
            source, target, send, recv,
            device_id=(place, core if side is None else side), device_id_type=MESH)

    up = lax.rem(me + RING, count)
    down = lax.rem(me - RING + count, count)

    def peer(k):
        return me - spot + lax.rem(spot + k, RING)

    def step_to(k):
        return lax.rem(spot + k, RING) - spot

    def near_kv(h):
        return remote(window.at[h, DEPTH], window.at[h, RING], kv_send.at[h, 0], kv_recv.at[h, RING], up)

    def far_kv(h):
        return remote(window.at[h, RING], window.at[h, 0], kv_send.at[h, 1], kv_recv.at[h, 0], up)

    def ring_kv(h, k, held, slot):
        which = 1 + k if held == RING else 4 + k
        return remote(window.at[h, held], window.at[h, slot], kv_send.at[h, which], kv_recv.at[h, slot], peer(k))

    def arrival(h, slot):
        return remote(window.at[h, slot], window.at[h, slot], kv_send.at[h, 0], kv_recv.at[h, slot], up)

    def first_copy(h, k):
        return remote(partial.at[h, RING + step_to(k)], first_in.at[h, k - 1],
                      first_send.at[h, k - 1], first_recv.at[h, k - 1], peer(k))

    def second_copy(h, k):
        slot = jnp.where(step_to(k) > 0, step_to(k), DEPTH + step_to(k))
        return remote(partial.at[h, slot], second_in.at[h, k - 1],
                      second_send.at[h, k - 1], second_recv.at[h, k - 1], peer(k))

    def far_copy(h):
        return remote(far_out.at[h], far_in.at[h], far_send.at[h], far_recv.at[h], down)

    def near_copy(h):
        return remote(near_out.at[h], near_in.at[h], near_send.at[h], near_recv.at[h], down)

    def g_copy(h):
        return remote(grad_ref.at[:, lanes(other + h * width, width)],
                      g_heads.at[my_rows, lanes(h * width, width)], g_send.at[h], g_recv.at[h], me, 1 - core)

    def o_copy(h):
        return remote(o_heads.at[other_rows, lanes(h * width, width)],
                      o_arrived.at[:, lanes(h * width, width)], o_send.at[h], o_recv.at[h], me, 1 - core)

    def greet(place, side):
        pl.semaphore_signal(barrier, inc=1, device_id=(place, side), device_id_type=MESH)

    barrier = pltpu.get_barrier_semaphore()
    greet(me, 1 - core)
    for k in range(1, RING):
        greet(peer(k), core)
    pl.when(above)(lambda: greet(up, core))
    pl.when(below)(lambda: greet(down, core))

    for h in range(heads):
        window[h, DEPTH, 0] = key_ref[:, h * HEAD_DIM : (h + 1) * HEAD_DIM]
        window[h, DEPTH, 1] = value_ref[:, h * HEAD_DIM : (h + 1) * HEAD_DIM]
    for d in range(1, SPAN):
        @pl.when(me < d)
        def _():
            window[:, DEPTH - d] = jnp.zeros((heads,) + window.shape[2:], jnp.bfloat16)

    pl.semaphore_wait(barrier, RING + jnp.where(below, 1, 0) + jnp.where(above, 1, 0))

    def send_out(h, carry):
        pl.when(above)(lambda: near_kv(h).start())
        g_copy(h).start()
        return carry

    def send_own(h, wait=False):
        for k in range(1, RING):
            @pl.when(step_to(k) > 0)
            def _():
                copy = ring_kv(h, k, DEPTH, DEPTH - step_to(k))
                copy.wait_send() if wait else copy.start()

    def send_near(h, wait=False):
        @pl.when(below)
        def _():
            for k in range(1, RING):
                copy = ring_kv(h, k, RING, RING - step_to(k))
                copy.wait_send() if wait else copy.start()

    def send_far(h, wait=False):
        @pl.when(two_below)
        def _():
            if not wait:
                arrival(h, 0).wait_recv()
            for k in range(1, RING):
                @pl.when(step_to(k) < 0)
                def _():
                    copy = ring_kv(h, k, 0, -step_to(k))
                    copy.wait_send() if wait else copy.start()

    def relay(h, carry):
        @pl.when(below)
        def _():
            arrival(h, RING).wait_recv()
            pl.when(above)(lambda: far_kv(h).start())
        return carry

    def spread(h):
        send_own(h)
        send_near(h)
        send_far(h)

    lax.fori_loop(0, heads, send_out, 0)
    g_heads[my_rows, :] = grad_ref[:, lanes(mine, columns)]
    fill_constants(seg_ref, me, tmp)
    lax.fori_loop(0, heads, relay, 0)
    spread(0)

    def merge_far(h):
        @pl.when(two_below)
        def _():
            total[...] = partial[h, 0].astype(jnp.float32)
            for k in range(1, RING):
                @pl.when(spot >= k)
                def _():
                    second_copy(h, k).wait_recv()
                    total[...] += second_in[h, k - 1].astype(jnp.float32)
            far_out[h] = total[...].astype(jnp.bfloat16)
            far_copy(h).start()

    def merge_near(h):
        @pl.when(below)
        def _():
            total[...] = partial[h, RING].astype(jnp.float32)
            for k in range(1, RING):
                first_copy(h, k).wait_recv()
                total[...] += first_in[h, k - 1].astype(jnp.float32)

            @pl.when(above)
            def _():
                far_copy(h).wait_recv()
                total[...] += far_in[h].astype(jnp.float32)
            near_out[h] = total[...].astype(jnp.bfloat16)
            near_copy(h).start()

    def head_step(h, carry):
        pl.when(h + 1 < heads)(lambda: spread(h + 1))
        g_copy(h).wait_recv()
        for d in range(1, SPAN):
            if d % RING:
                @pl.when(me >= d)
                def _():
                    arrival(h, DEPTH - d).wait_recv()

        def at(ref, g):
            return ref[:, lanes(h * width + g * HEAD_DIM, HEAD_DIM)]

        def put(ref, g, value):
            ref[:, lanes(h * width + g * HEAD_DIM, HEAD_DIM)] = value

        def put_block(which, j, value):
            partial[h, j, which] = value

        attend_group(
            functools.partial(at, q_ref),
            functools.partial(at, g_heads),
            lambda j: window[h, j, 0],
            lambda j: window[h, j, 1],
            functools.partial(put, o_heads),
            functools.partial(put, dq_ref),
            functools.partial(put_block, 0),
            functools.partial(put_block, 1),
            tmp,
        )
        for k in range(1, RING):
            pl.when(below)(lambda: first_copy(h, k).start())
            pl.when((step_to(k) < 0) | two_below)(lambda: second_copy(h, k).start())
        o_copy(h).start()
        out_ref[:, lanes(mine + h * width, width)] = o_heads[my_rows, lanes(h * width, width)]
        pl.when(h >= 1)(lambda: merge_far(h - 1))
        pl.when(h >= 2)(lambda: merge_near(h - 2))
        return carry

    lax.fori_loop(0, heads, head_step, 0)
    merge_far(heads - 1)
    if heads > 1:
        merge_near(heads - 2)
    merge_near(heads - 1)

    def finish_head(h, carry):
        total[...] = partial[h, DEPTH].astype(jnp.float32)
        for k in range(1, RING):
            @pl.when(spot < k)
            def _():
                second_copy(h, k).wait_recv()
                total[...] += second_in[h, k - 1].astype(jnp.float32)

        @pl.when(above)
        def _():
            near_copy(h).wait_recv()
            total[...] += near_in[h].astype(jnp.float32)
        dk_ref[:, lanes(h * HEAD_DIM, HEAD_DIM)] = total[0].astype(jnp.bfloat16)
        dv_ref[:, lanes(h * HEAD_DIM, HEAD_DIM)] = total[1].astype(jnp.bfloat16)

        g_copy(h).wait_send()
        o_copy(h).wait()
        send_own(h, wait=True)
        send_near(h, wait=True)
        send_far(h, wait=True)
        for k in range(1, RING):
            pl.when(below)(lambda: first_copy(h, k).wait_send())
            pl.when((step_to(k) < 0) | two_below)(lambda: second_copy(h, k).wait_send())
        pl.when(above)(lambda: near_kv(h).wait_send())
        pl.when(above & below)(lambda: far_kv(h).wait_send())
        pl.when(below)(lambda: near_copy(h).wait_send())
        pl.when(two_below)(lambda: far_copy(h).wait_send())
        return carry

    lax.fori_loop(0, heads, finish_head, 0)
    out_ref[:, lanes(other, columns)] = o_arrived[...]


def attention(count, queries, grad_out, keys, values, segments):
    rows, columns = queries.shape
    heads = keys.shape[1] // HEAD_DIM
    half = grad_out.shape[0]
    tile = (2, rows, HEAD_DIM)
    in_vmem = pl.BlockSpec(memory_space=pltpu.VMEM)
    blocks = [(SPAN,), (SPAN,), (RING - 1,), (RING - 1,), (), (), (), ()]
    counts = [DEPTH, SPAN] + [RING - 1] * 4
    return pl.pallas_call(
        functools.partial(kernel, count),
        in_specs=[in_vmem] * 5,
        out_specs=[in_vmem] * 4,
        out_shape=[jax.ShapeDtypeStruct(a.shape, jnp.bfloat16) for a in (grad_out, queries, keys, values)],
        scratch_shapes=[pltpu.VMEM((heads,) + b + tile, jnp.bfloat16) for b in blocks]
        + [
            pltpu.VMEM(tile, jnp.float32),
            pltpu.VMEM((rows, columns), jnp.bfloat16),
            pltpu.VMEM((rows, columns), jnp.bfloat16),
            pltpu.VMEM((half, columns), jnp.bfloat16),
        ]
        + [pltpu.SemaphoreType.DMA((heads, n)) for n in counts]
        + [pltpu.SemaphoreType.DMA((heads,))] * 8
        + scratch(rows),
        compiler_params=pltpu.CompilerParams(
            vmem_limit_bytes=56 * 1024 * 1024, collective_id=0, has_side_effects=True),
        name="attention",
    )(queries, grad_out, keys, values, segments)


def body(queries, keys, values, grad_out, segments):
    by_block = segments.reshape(-1, queries.shape[0])
    return tuple(attention(lax.axis_size("dp"), queries, grad_out, keys, values, by_block))


def solution(mesh):
    placed = (P("dp", "head"), P("dp", "head"), P("dp", "head"), P(("dp", "head"), None), P())
    return jax.shard_map(
        body,
        mesh=mesh,
        in_specs=placed,
        out_specs=(P(("dp", "head"), None), P("dp", "head"), P("dp", "head"), P("dp", "head")),
        check_vma=False,
    )
```

time: 118 us -> 84.5 us (0.72)
  the two profiles are of different devices: /device:TPU:0 before, /device:TPU:12 now
where the time goes in v3:
time: 84.5 us; the launch traced here: 84.3 us
  Pallas kernels  78.5 us (93%)
  local copies, waits for them, and re-layouts  5.23 us (6%)
    pallas_call x1, Pallas kernels, attention(): pl.pallas_call(functools.partial(kernel, count), in_specs=[in_vmem] * 5,...  78.5 us
    unnamed x10, local copies, waits for them, and re-layouts  5.23 us

profile of v3, /device:TPU:12, one launch (start us, length us, event | category | flops | bytes accessed | tf_op | source)
XLA Modules:
  0.0 84.3 jit_solution(13114199033933508742)
XLA Ops:
  0.6 78.5 %attention.1 = (bf16[64,12288]{1,0:T(8,128)(2,1)}, bf16[128,6144]{1,0:T(8,128)(2,1)}, bf16[128,512]{1,0:T(8,128)(2,1)}, bf16[128,512]{1,0:T(8,128)(2,1)}) custom-call(bf16[128,6144]{1,0:T(8,128)(2,1)} %q_ref.1, bf16[64,12288]{1,0:T(8,128)(2,1)} %grad_ref.1, bf16[128,512]{1,0:T(8,128)(2,1)} %key_ref.1, bf16[128,512]{1,0:T(8,128)(2,1)} %value_ref.1, ...), custom_call_target="tpu_custom_call" | custom-call | tf_op jit(solution)/shard_map/attention/pallas_call | solution.py:416
  79.1 0.0 copy-start
  79.1 2.8 %copy.13 = bf16[64,12288]{1,0:T(8,128)(2,1)} copy(bf16[64,12288]{1,0:T(8,128)(2,1)} %get-tuple-element.8) | data formatting | bytes 3145728
  81.9 0.0 copy-done
  81.9 0.0 copy-start.2
  81.9 0.0 copy-start.1
  81.9 1.1 %copy.14 = bf16[128,6144]{1,0:T(8,128)(2,1)} copy(bf16[128,6144]{1,0:T(8,128)(2,1)S(1)} %copy-done) | data formatting | bytes 3145728
  83.0 0.0 copy-done.2
  83.0 0.7 copy.15
  83.7 0.0 copy-done.1
  83.7 0.7 copy.16
Async XLA Ops:
  79.1 2.8 %copy-start = (bf16[128,6144]{1,0:T(8,128)(2,1)S(1)}, bf16[128,6144]{1,0:T(8,128)(2,1)}, u32[]{:S(2)}) copy-start(bf16[128,6144]{1,0:T(8,128)(2,1)} %get-tuple-element.9) | copy-start | bytes 4718596
  81.9 1.1 %copy-start.2 = (bf16[128,512]{1,0:T(8,128)(2,1)S(1)}, bf16[128,512]{1,0:T(8,128)(2,1)}, u32[]{:S(2)}) copy-start(bf16[128,512]{1,0:T(8,128)(2,1)} %get-tuple-element.10) | copy-start | bytes 393220
  81.9 1.8 %copy-start.1 = (bf16[128,512]{1,0:T(8,128)(2,1)S(1)}, bf16[128,512]{1,0:T(8,128)(2,1)}, u32[]{:S(2)}) copy-start(bf16[128,512]{1,0:T(8,128)(2,1)} %get-tuple-element.11) | copy-start | bytes 393220

commit v4 on v3

--- a/solution.py
+++ b/solution.py
@@ -15,6 +15,7 @@
 SPAN = DEPTH + 1
 RING = DEPTH // 2
 GROUP = QHEADS // KVHEADS
+PAIRS = GROUP // 2
 MASKED = -(2.0**100)
 SCALE = 1.0 / math.sqrt(HEAD_DIM)
 NT = (((1,), (1,)), ((), ()))
@@ -28,7 +29,7 @@
     return lax.dot_general(a, b, NT, preferred_element_type=jnp.float32)
 
 
-def attend_group(q_at, g_at, k_at, v_at, put_out, put_dq, put_dk, put_dv, tmp):
+def attend_group(q_at, g_at, k_at, v_at, put_out, put_dq, put_dk, put_dv, stored, tmp):
     (k_aug, v_aug, k_t, v_t, q_aug, g_aug, q_norm, g_norm, p_all, ds_all) = tmp[:10]
     scores, slopes = tmp[10:12], tmp[12:14]
     rows = HEAD_DIM
@@ -47,69 +48,77 @@
     two = 2 * rows
     lane = lax.broadcasted_iota(jnp.int32, (two, HEAD_DIM), 1)
 
-    def quad_step(i, carry):
-        at = [slice(t * two, (t + 1) * two) for t in range(2)]
-        inv_t = [None, None]
-
-        def softmax(t):
-            score = scores[t]
-            top = score[0:rows, :].reshape(rows // 8, 8, two).max(axis=0)
-            for j in range(1, SPAN):
-                part = score[j * rows : (j + 1) * rows, :]
-                top = jnp.maximum(top, part.reshape(rows // 8, 8, two).max(axis=0))
-            top = jnp.max(top, axis=0, keepdims=True)
-            for j in range(SPAN):
-                part = score[j * rows : (j + 1) * rows, :]
-                e = jnp.exp2((part - top) * (SCALE * math.log2(math.e)))
-                p_all[i, j * rows : (j + 1) * rows, at[t]] = e.astype(jnp.bfloat16)
-
-        def output(t):
-            both = dot(v_t[...], p_all[i, :, at[t]])
-            inv = 1.0 / both[HEAD_DIM : HEAD_DIM + 1]
-            inv_t[t] = jnp.broadcast_to(inv, (HEAD_DIM, two)).T
-            out = (both[:HEAD_DIM].T * inv_t[t]).astype(jnp.bfloat16)
-            put_out(4 * i + 2 * t, out[:rows])
-            put_out(4 * i + 2 * t + 1, out[rows:])
-            g_pair = g_aug[i, at[t], :HEAD_DIM].astype(jnp.float32)
-            delta = -jnp.sum(g_pair * out.astype(jnp.float32), axis=1, keepdims=True)
-            hi = delta.astype(jnp.bfloat16).astype(jnp.float32)
-            mid = (delta - hi).astype(jnp.bfloat16).astype(jnp.float32)
-            low = delta - hi - mid
-            tail = jnp.where(lane == 0, hi, jnp.where(lane == 1, mid, jnp.where(lane == 2, low, 0.0)))
-            g_aug[i, at[t], HEAD_DIM:] = tail.astype(jnp.bfloat16)
-            q_pair = q_aug[i, at[t], :HEAD_DIM].astype(jnp.float32)
-            q_norm[i, at[t], :] = (q_pair * inv_t[t]).astype(jnp.bfloat16)
-            g_norm[i, at[t], :] = (g_pair * inv_t[t]).astype(jnp.bfloat16)
-
-        def grad_weights(t):
-            slopes[t][...] = dot_nt(v_aug[...], g_aug[i, at[t], :])
-
-        def grad_scores(t):
-            for j in range(SPAN):
-                keys = slice(j * rows, (j + 1) * rows)
-                slope = slopes[t][keys, :].astype(jnp.bfloat16)
-                ds_all[i, keys, at[t]] = p_all[i, keys, at[t]] * slope
-
-        def grad_query(t):
-            dq = (dot(k_t[...], ds_all[i, :, at[t]]).T * (inv_t[t] * SCALE)).astype(jnp.bfloat16)
-            put_dq(4 * i + 2 * t, dq[:rows])
-            put_dq(4 * i + 2 * t + 1, dq[rows:])
-
-        scores[0][...] = dot_nt(k_aug[...], q_aug[i, at[0], :])
-        softmax(0)
-        scores[1][...] = dot_nt(k_aug[...], q_aug[i, at[1], :])
-        output(0)
-        softmax(1)
-        grad_weights(0)
-        output(1)
-        grad_scores(0)
-        grad_weights(1)
-        grad_query(0)
-        grad_scores(1)
-        grad_query(1)
-        return carry
-
-    lax.fori_loop(0, GROUP // 4, quad_step, 0)
+    def place(t):
+        return t // 2, slice(t % 2 * two, (t % 2 + 1) * two)
+
+    inv_t = [None] * PAIRS
+
+    def softmax(t):
+        i, at = place(t)
+        score = scores[t % 2]
+        top = score[0:rows, :].reshape(rows // 8, 8, two).max(axis=0)
+        for j in range(1, SPAN):
+            part = score[j * rows : (j + 1) * rows, :]
+            top = jnp.maximum(top, part.reshape(rows // 8, 8, two).max(axis=0))
+        top = jnp.max(top, axis=0, keepdims=True)
+        for j in range(SPAN):
+            part = score[j * rows : (j + 1) * rows, :]
+            e = jnp.exp2((part - top) * (SCALE * math.log2(math.e)))
+            p_all[i, j * rows : (j + 1) * rows, at] = e.astype(jnp.bfloat16)
+
+    def output(t):
+        i, at = place(t)
+        both = dot(v_t[...], p_all[i, :, at])
+        inv = 1.0 / both[HEAD_DIM : HEAD_DIM + 1]
+        inv_t[t] = jnp.broadcast_to(inv, (HEAD_DIM, two)).T
+        out = (both[:HEAD_DIM].T * inv_t[t]).astype(jnp.bfloat16)
+        put_out(2 * t, out[:rows])
+        put_out(2 * t + 1, out[rows:])
+        g_pair = g_aug[i, at, :HEAD_DIM].astype(jnp.float32)
+        delta = -jnp.sum(g_pair * out.astype(jnp.float32), axis=1, keepdims=True)
+        hi = delta.astype(jnp.bfloat16).astype(jnp.float32)
+        mid = (delta - hi).astype(jnp.bfloat16).astype(jnp.float32)
+        low = delta - hi - mid
+        tail = jnp.where(lane == 0, hi, jnp.where(lane == 1, mid, jnp.where(lane == 2, low, 0.0)))
+        g_aug[i, at, HEAD_DIM:] = tail.astype(jnp.bfloat16)
+        q_pair = q_aug[i, at, :HEAD_DIM].astype(jnp.float32)
+        q_norm[i, at, :] = (q_pair * inv_t[t]).astype(jnp.bfloat16)
+        g_norm[i, at, :] = (g_pair * inv_t[t]).astype(jnp.bfloat16)
+
+    def grad_weights(t):
+        i, at = place(t)
+        slopes[t % 2][...] = dot_nt(v_aug[...], g_aug[i, at, :])
+
+    def grad_scores(t):
+        i, at = place(t)
+        for j in range(SPAN):
+            keys = slice(j * rows, (j + 1) * rows)
+            slope = slopes[t % 2][keys, :].astype(jnp.bfloat16)
+            ds_all[i, keys, at] = p_all[i, keys, at] * slope
+
+    def grad_query(t):
+        i, at = place(t)
+        dq = (dot(k_t[...], ds_all[i, :, at]).T * (inv_t[t] * SCALE)).astype(jnp.bfloat16)
+        put_dq(2 * t, dq[:rows])
+        put_dq(2 * t + 1, dq[rows:])
+
+    def raw_scores(t):
+        i, at = place(t)
+        scores[t % 2][...] = dot_nt(k_aug[...], q_aug[i, at, :])
+
+    raw_scores(0)
+    for t in range(PAIRS):
+        if t + 1 < PAIRS:
+            raw_scores(t + 1)
+        softmax(t)
+        if t > 0:
+            grad_scores(t - 1)
+        output(t)
+        grad_weights(t)
+        if t > 0:
+            grad_query(t - 1)
+    grad_scores(PAIRS - 1)
+    grad_query(PAIRS - 1)
     for j in range(0, SPAN, 3):
         keys = slice(j * rows, (j + 3) * rows)
         dk = sum(dot(ds_all[i, keys, :], q_norm[i]) for i in range(GROUP // 4))
@@ -117,6 +126,7 @@
         for b in range(3):
             put_dk(j + b, (SCALE * dk[b * rows : (b + 1) * rows]).astype(jnp.bfloat16))
             put_dv(j + b, dv[b * rows : (b + 1) * rows].astype(jnp.bfloat16))
+        stored(j, j + 3)
 
 
 def block_mask(seg_ref, me, j):
@@ -165,9 +175,10 @@
 
 def kernel(count, q_ref, grad_ref, key_ref, value_ref, seg_ref, out_ref, dq_ref, dk_ref, dv_ref,
            window, partial, first_in, second_in, far_out, far_in, near_out, near_in, total,
-           g_heads, o_heads, o_arrived,
+           q_heads, g_heads, o_heads, dq_heads,
            kv_send, kv_recv, first_send, first_recv, second_send, second_recv,
-           far_send, far_recv, near_send, near_recv, g_send, g_recv, o_send, o_recv, *tmp):
+           far_send, far_recv, near_send, near_recv, g_send, g_recv, o_send, o_recv,
+           own_sem, dq_sem, in_sem, *tmp):
     me, core = lax.axis_index("dp"), lax.axis_index("head")
     spot = lax.rem(me, RING)
     heads = window.shape[0]
@@ -231,11 +242,24 @@
 
     def o_copy(h):
         return remote(o_heads.at[other_rows, lanes(h * width, width)],
-                      o_arrived.at[:, lanes(h * width, width)], o_send.at[h], o_recv.at[h], me, 1 - core)
+                      out_ref.at[:, lanes(mine + h * width, width)], o_send.at[h], o_recv.at[h], me, 1 - core)
+
+    def own_out(h):
+        return pltpu.make_async_copy(o_heads.at[my_rows, lanes(h * width, width)],
+                                     out_ref.at[:, lanes(mine + h * width, width)], own_sem.at[h])
+
+    def dq_out(h):
+        part = (slice(None), lanes(h * width, width))
+        return pltpu.make_async_copy(dq_heads.at[part], dq_ref.at[part], dq_sem.at[h])
+
+    q_in = pltpu.make_async_copy(q_ref, q_heads, in_sem.at[0])
+    g_in = pltpu.make_async_copy(grad_ref.at[:, lanes(mine, columns)], g_heads.at[my_rows, :], in_sem.at[1])
 
     def greet(place, side):
         pl.semaphore_signal(barrier, inc=1, device_id=(place, side), device_id_type=MESH)
 
+    g_in.start()
+    q_in.start()
     barrier = pltpu.get_barrier_semaphore()
     greet(me, 1 - core)
     for k in range(1, RING):
@@ -296,10 +320,11 @@
         send_far(h)
 
     lax.fori_loop(0, heads, send_out, 0)
-    g_heads[my_rows, :] = grad_ref[:, lanes(mine, columns)]
     fill_constants(seg_ref, me, tmp)
     lax.fori_loop(0, heads, relay, 0)
     spread(0)
+    g_in.wait()
+    q_in.wait()
 
     def merge_far(h):
         @pl.when(two_below)
@@ -346,31 +371,39 @@
         def put_block(which, j, value):
             partial[h, j, which] = value
 
+        def send_slots(start, stop):
+            for slot in range(start, stop):
+                k = slot % RING
+                if k == 0:
+                    continue
+                ahead = step_to(k) > 0
+                if slot < RING:
+                    pl.when(ahead & two_below)(lambda: second_copy(h, k).start())
+                    pl.when(jnp.logical_not(ahead) & below)(lambda: first_copy(h, k).start())
+                else:
+                    pl.when(ahead & below)(lambda: first_copy(h, k).start())
+                    pl.when(jnp.logical_not(ahead))(lambda: second_copy(h, k).start())
+
         attend_group(
-            functools.partial(at, q_ref),
+            functools.partial(at, q_heads),
             functools.partial(at, g_heads),
             lambda j: window[h, j, 0],
             lambda j: window[h, j, 1],
             functools.partial(put, o_heads),
-            functools.partial(put, dq_ref),
+            functools.partial(put, dq_heads),
             functools.partial(put_block, 0),
             functools.partial(put_block, 1),
+            send_slots,
             tmp,
         )
-        for k in range(1, RING):
-            pl.when(below)(lambda: first_copy(h, k).start())
-            pl.when((step_to(k) < 0) | two_below)(lambda: second_copy(h, k).start())
         o_copy(h).start()
-        out_ref[:, lanes(mine + h * width, width)] = o_heads[my_rows, lanes(h * width, width)]
+        own_out(h).start()
+        dq_out(h).start()
         pl.when(h >= 1)(lambda: merge_far(h - 1))
         pl.when(h >= 2)(lambda: merge_near(h - 2))
         return carry
 
     lax.fori_loop(0, heads, head_step, 0)
-    merge_far(heads - 1)
-    if heads > 1:
-        merge_near(heads - 2)
-    merge_near(heads - 1)
 
     def finish_head(h, carry):
         total[...] = partial[h, DEPTH].astype(jnp.float32)
@@ -388,7 +421,12 @@
         dv_ref[:, lanes(h * HEAD_DIM, HEAD_DIM)] = total[1].astype(jnp.bfloat16)
 
         g_copy(h).wait_send()
-        o_copy(h).wait()
+        o_copy(h).wait_send()
+        remote(o_heads.at[other_rows, lanes(h * width, width)],
+               out_ref.at[:, lanes(other + h * width, width)],
+               o_send.at[h], o_recv.at[h], me, 1 - core).wait_recv()
+        own_out(h).wait()
+        dq_out(h).wait()
         send_own(h, wait=True)
         send_near(h, wait=True)
         send_far(h, wait=True)
@@ -401,32 +439,36 @@
         pl.when(two_below)(lambda: far_copy(h).wait_send())
         return carry
 
-    lax.fori_loop(0, heads, finish_head, 0)
-    out_ref[:, lanes(other, columns)] = o_arrived[...]
+    early = max(heads - 2, 0)
+    if heads > 1:
+        merge_near(heads - 2)
+    lax.fori_loop(0, early, finish_head, 0)
+    merge_far(heads - 1)
+    merge_near(heads - 1)
+    lax.fori_loop(early, heads, finish_head, 0)
 
 
 def attention(count, queries, grad_out, keys, values, segments):
     rows, columns = queries.shape
     heads = keys.shape[1] // HEAD_DIM
-    half = grad_out.shape[0]
     tile = (2, rows, HEAD_DIM)
     in_vmem = pl.BlockSpec(memory_space=pltpu.VMEM)
+    in_place = pl.BlockSpec(memory_space=pl.ANY)
     blocks = [(SPAN,), (SPAN,), (RING - 1,), (RING - 1,), (), (), (), ()]
     counts = [DEPTH, SPAN] + [RING - 1] * 4
     return pl.pallas_call(
         functools.partial(kernel, count),
-        in_specs=[in_vmem] * 5,
-        out_specs=[in_vmem] * 4,
+        in_specs=[in_place] * 2 + [in_vmem] * 3,
+        out_specs=[in_place] * 2 + [in_vmem] * 2,
         out_shape=[jax.ShapeDtypeStruct(a.shape, jnp.bfloat16) for a in (grad_out, queries, keys, values)],
         scratch_shapes=[pltpu.VMEM((heads,) + b + tile, jnp.bfloat16) for b in blocks]
         + [
             pltpu.VMEM(tile, jnp.float32),
-            pltpu.VMEM((rows, columns), jnp.bfloat16),
-            pltpu.VMEM((rows, columns), jnp.bfloat16),
-            pltpu.VMEM((half, columns), jnp.bfloat16),
         ]
+        + [pltpu.VMEM((rows, columns), jnp.bfloat16)] * 4
         + [pltpu.SemaphoreType.DMA((heads, n)) for n in counts]
-        + [pltpu.SemaphoreType.DMA((heads,))] * 8
+        + [pltpu.SemaphoreType.DMA((heads,))] * 10
+        + [pltpu.SemaphoreType.DMA((2,))]
         + scratch(rows),
         compiler_params=pltpu.CompilerParams(
             vmem_limit_bytes=56 * 1024 * 1024, collective_id=0, has_side_effects=True),

time: 84.5 us -> 80.9 us (0.957)
  the two profiles are of different devices: /device:TPU:12 before, /device:TPU:0 now
where the time goes in v4:
time: 80.9 us; the launch traced here: 80.8 us
  Pallas kernels  74.9 us (93%)
  local copies, waits for them, and re-layouts  5.23 us (6%)
    pallas_call x1, Pallas kernels, attention(): pl.pallas_call(functools.partial(kernel, count), in_specs=[in_place] * 2...  74.9 us
    unnamed x10, local copies, waits for them, and re-layouts  5.23 us

profile of v4, /device:TPU:0, one launch (start us, length us, event | category | flops | bytes accessed | tf_op | source)
XLA Modules:
  0.0 80.8 jit_solution(13983844460701617235)
XLA Ops:
  0.6 74.9 %attention.1 = (bf16[64,12288]{1,0:T(8,128)(2,1)}, bf16[128,6144]{1,0:T(8,128)(2,1)}, bf16[128,512]{1,0:T(8,128)(2,1)}, bf16[128,512]{1,0:T(8,128)(2,1)}) custom-call(bf16[128,6144]{1,0:T(8,128)(2,1)} %q_ref.1, bf16[64,12288]{1,0:T(8,128)(2,1)} %grad_ref.1, bf16[128,512]{1,0:T(8,128)(2,1)} %key_ref.1, bf16[128,512]{1,0:T(8,128)(2,1)} %value_ref.1, ...), custom_call_target="tpu_custom_call" | custom-call | tf_op jit(solution)/shard_map/attention/pallas_call | solution.py:459
  75.5 0.0 copy-start
  75.6 2.8 %copy.13 = bf16[64,12288]{1,0:T(8,128)(2,1)} copy(bf16[64,12288]{1,0:T(8,128)(2,1)} %get-tuple-element.8) | data formatting | bytes 3145728
  78.3 0.0 copy-done
  78.3 0.0 copy-start.2
  78.3 0.0 copy-start.1
  78.3 1.1 %copy.14 = bf16[128,6144]{1,0:T(8,128)(2,1)} copy(bf16[128,6144]{1,0:T(8,128)(2,1)S(1)} %copy-done) | data formatting | bytes 3145728
  79.5 0.0 copy-done.2
  79.5 0.7 copy.15
  80.1 0.0 copy-done.1
  80.1 0.7 copy.16
Async XLA Ops:
  75.5 2.8 %copy-start = (bf16[128,6144]{1,0:T(8,128)(2,1)S(1)}, bf16[128,6144]{1,0:T(8,128)(2,1)}, u32[]{:S(2)}) copy-start(bf16[128,6144]{1,0:T(8,128)(2,1)} %get-tuple-element.9) | copy-start | bytes 4718596
  78.3 1.1 %copy-start.2 = (bf16[128,512]{1,0:T(8,128)(2,1)S(1)}, bf16[128,512]{1,0:T(8,128)(2,1)}, u32[]{:S(2)}) copy-start(bf16[128,512]{1,0:T(8,128)(2,1)} %get-tuple-element.10) | copy-start | bytes 393220
  78.3 1.8 %copy-start.1 = (bf16[128,512]{1,0:T(8,128)(2,1)S(1)}, bf16[128,512]{1,0:T(8,128)(2,1)}, u32[]{:S(2)}) copy-start(bf16[128,512]{1,0:T(8,128)(2,1)} %get-tuple-element.11) | copy-start | bytes 393220
